TPU v7x, 512 devices: a whole 4x8x8 slice. The times are simulated.
512 devices in a mesh: worker: 64 (over y, z), tensor: 8 (over x, core).
Axes of the slice: x: 4, y: 8, z: 8, core: 2. Of those that a mesh axis runs over, the one named last changes fastest.
Arguments:
- queries: bfloat16 [256, 256, 1024], P('worker', None, 'tensor'), may hold values from -6 to 6
- key_heads: bfloat16 [256, 256, 1024], P('worker', None, 'tensor'), may hold values from -6 to 6
- values_in: bfloat16 [256, 256, 2048], P('worker', None, 'tensor'), may hold values from -6 to 6
- out_gate: bfloat16 [256, 256, 2048], P('worker', None, 'tensor'), may hold values from -6 to 6
- log_decay: float32 [256, 16, 256], P('worker', 'tensor'), may hold values from -1 to 0
- write_rate: float32 [256, 16, 256], P('worker', 'tensor'), may hold values from 0.5 to 0.95
- cache_states: float32 [768, 16, 128, 128], P('worker', 'tensor'), may hold values from -6 to 6
- norm_gain: float32 [128], replicated, may hold values from 0.1 to 1.9
- out_proj: bfloat16 [2048, 2048], P('tensor'), may hold values from -0.125 to 0.125
- hit_owner: int32 [256], P('worker'), may hold values from 0 to 63, as said below
- hit_node: int32 [256], P('worker'), may hold values from 0 to 11
- prefix_len: int32 [256], P('worker'), may hold values from 0 to 768, as said below
- write_slot: int32 [256], P('worker'), may hold values from 0 to 255, as said below
Outputs:
- mixed: bfloat16 [256, 256, 2048], P('worker', None, 'tensor')
- end_states: float32 [256, 16, 128, 128], P('worker', 'tensor')
Inputs may be any that keep to these rules, and one draw needn't show every extreme that they name: `hit_owner`: the worker at most 2 positions away from the request's own worker along the worker axis, counted around the end (the first worker follows the last); all of one worker's requests may name workers at the same distance. `prefix_len`: a multiple of 256; 0 where nothing is cached, and hit_owner and hit_node are then unused. A permutation of 0 to 255; row write_slot[r] lies on worker write_slot[r] // 4, at most 2 positions away from request r's worker, counted around the end.
All inputs are finite; a program needn't handle non-finite values.
Results may differ from a plain program's by a relative error of at most 0.017.
Values may be sent and summed in bfloat16 or wider, within the bound.
A program may use at most 64 MiB of HBM per device.

v0:
```python
import jax
import jax.numpy as jnp
from jax import lax
from jax.sharding import PartitionSpec as P

DK = 128
DV = 128
REACH = 2


def shifted(x, axis, by):
    devices = lax.axis_size(axis)
    return lax.ppermute(x, axis, [(i, (i + by) % devices) for i in range(devices)])


def unit_rows(matrix):
    return matrix * lax.rsqrt(jnp.sum(matrix * matrix, axis=-1, keepdims=True) + 1e-06)


def exact_dot(equation, first_operand, second_operand):
    return jnp.einsum(equation, first_operand, second_operand, precision=lax.Precision.HIGHEST)


def block_dot(equation, first_operand, second_operand):
    return jnp.einsum(equation, first_operand, second_operand, precision=lax.Precision.HIGH)


def delta_block(running_state, query_blk, key_blk, value_blk, decay_blk, rate_blk):
    block_size = decay_blk.shape[-1]
    running = jnp.cumsum(decay_blk, axis=-1)
    row_ids = lax.broadcasted_iota(jnp.int32, (block_size, block_size), 0)
    col_ids = lax.broadcasted_iota(jnp.int32, (block_size, block_size), 1)
    causal = row_ids >= col_ids
    strict = row_ids > col_ids
    spread = running[..., :, None] - running[..., None, :]
    within = jnp.where(causal, jnp.exp(jnp.where(causal, spread, 0.0)), 0.0)
    intersection = block_dot("rhik,rhjk->rhij", key_blk, key_blk)
    system = jnp.where(strict, rate_blk[..., :, None] * within * intersection, 0.0) + jnp.eye(
        block_size, dtype=jnp.float32
    )
    from_start = jnp.exp(running)
    stacked = jnp.concatenate(
        [rate_blk[..., None] * value_blk, (rate_blk * from_start)[..., None] * key_blk], axis=-1
    )
    solved = lax.linalg.triangular_solve(
        system, stacked, left_side=True, lower=True, unit_diagonal=True
    )
    value_dim = value_blk.shape[-1]
    fresh_values = solved[..., :value_dim] - exact_dot(
        "rhbk,rhkv->rhbv", solved[..., value_dim:], running_state
    )
    scores = block_dot("rhik,rhjk->rhij", query_blk, key_blk) * within
    outputs = from_start[..., None] * exact_dot(
        "rhbk,rhkv->rhbv", query_blk, running_state
    ) + block_dot("rhij,rhjv->rhiv", scores, fresh_values)
    final_log = running[..., -1:]
    carried = jnp.exp(final_log - running)[..., None] * key_blk
    running_state = jnp.exp(final_log)[..., None] * running_state + exact_dot(
        "rhbk,rhbv->rhkv", carried, fresh_values
    )
    return (running_state, outputs)


def on_device(
    queries,
    key_heads,
    values_in,
    out_gate,
    log_decay,
    write_rate,
    cache_states,
    norm_gain,
    out_proj,
    hit_owner,
    hit_node,
    prefix_len,
    write_slot,
):
    requests_here = queries.shape[0]
    length = queries.shape[1]
    head_count = log_decay.shape[1]
    key_count = queries.shape[2] // DK
    head_group = head_count // key_count
    slot_count = cache_states.shape[0]
    workers = lax.axis_size("worker")
    worker_id = lax.axis_index("worker")
    query_unit = unit_rows(
        queries.astype(jnp.float32).reshape(requests_here, length, key_count, DK)
    ) * DK ** (-0.5)
    key_unit = unit_rows(
        key_heads.astype(jnp.float32).reshape(requests_here, length, key_count, DK)
    )
    query_unit = jnp.repeat(jnp.transpose(query_unit, (0, 2, 1, 3)), head_group, axis=1)
    key_unit = jnp.repeat(jnp.transpose(key_unit, (0, 2, 1, 3)), head_group, axis=1)
    value_heads = jnp.transpose(
        values_in.astype(jnp.float32).reshape(requests_here, length, head_count, DV), (0, 2, 1, 3)
    )
    cached = prefix_len > 0
    relative = (hit_owner - worker_id + workers + REACH) % workers - REACH
    pieces = []
    for offset in range(-REACH, REACH + 1):
        if offset == 0:
            pieces.append(cache_states)
        else:
            pieces.append(shifted(cache_states, "worker", -offset))
    window = jnp.concatenate(pieces, axis=0)
    start_state = jnp.take(window, (relative + REACH) * slot_count + hit_node, axis=0)
    start_state = jnp.where(cached[:, None, None, None], start_state, 0.0)
    block_size = min(128, length)
    running_state = start_state
    outputs = []
    for block_start in range(0, length, block_size):
        block_end = block_start + block_size
        running_state, block_out = delta_block(
            running_state,
            query_unit[:, :, block_start:block_end],
            key_unit[:, :, block_start:block_end],
            value_heads[:, :, block_start:block_end],
            log_decay[:, :, block_start:block_end],
            write_rate[:, :, block_start:block_end],
        )
        outputs.append(block_out)
    attended = jnp.concatenate(outputs, axis=2)
    gate_heads = jnp.transpose(
        out_gate.astype(jnp.float32).reshape(requests_here, length, head_count, DV), (0, 2, 1, 3)
    )
    scale_rows = lax.rsqrt(jnp.mean(attended * attended, axis=-1, keepdims=True) + 1e-06)
    normed = attended * scale_rows * norm_gain * jax.nn.silu(gate_heads)
    normed = (
        jnp.transpose(normed, (0, 2, 1, 3))
        .reshape(requests_here * length, head_count * DV)
        .astype(jnp.bfloat16)
    )
    partial_value = jnp.dot(normed, out_proj, preferred_element_type=jnp.float32).reshape(
        requests_here, length, out_proj.shape[1]
    )
    mixed = lax.psum_scatter(
        partial_value.astype(jnp.bfloat16), "tensor", scatter_dimension=2, tiled=True
    )
    target_worker = write_slot // requests_here
    target_lane = write_slot % requests_here
    target_move = (target_worker - worker_id + workers + REACH) % workers - REACH
    lane_ids = jnp.arange(requests_here, dtype=jnp.int32)
    end_states = jnp.zeros_like(running_state)
    for offset in range(-REACH, REACH + 1):
        routed = (target_move == offset)[:, None] & (target_lane[:, None] == lane_ids[None, :])
        packed = jnp.sum(
            jnp.where(routed[:, :, None, None, None], running_state[:, None], 0.0), axis=0
        )
        if offset != 0:
            packed = shifted(packed.astype(jnp.bfloat16), "worker", offset).astype(packed.dtype)
        end_states = end_states + packed
    return (mixed, end_states)


def solution(mesh):
    in_specs = (
        P("worker", None, "tensor"),
        P("worker", None, "tensor"),
        P("worker", None, "tensor"),
        P("worker", None, "tensor"),
        P("worker", "tensor", None),
        P("worker", "tensor", None),
        P("worker", "tensor", None, None),
        P(),
        P("tensor", None),
        P("worker"),
        P("worker"),
        P("worker"),
        P("worker"),
    )
    out_specs = (P("worker", None, "tensor"), P("worker", "tensor", None, None))
    return jax.shard_map(
        on_device, mesh=mesh, in_specs=in_specs, out_specs=out_specs, check_vma=False
    )
```

profile of v0, /device:TPU:1, one launch (start us, length us, event | category | flops | bytes accessed | tf_op | source)
XLA Modules:
  0.0 288.1 jit_solution(5571720502551016863)
XLA Ops:
  7.3 6.8 %collective-permute-start = (f32[12,2,128,128]{3,2,1,0:T(8,128)}, f32[12,2,128,128]{3,2,1,0:T(8,128)}, u32[]{:S(2)}, u32[]{:S(2)}) collective-permute-start(f32[12,2,128,128]{3,2,1,0:T(8,128)} %param.21), channel_id=1, source_target_pairs={{0,16},{8,24},{16,32},{24,40},{32,48},{40,56},{48,64},{56,72},{64,... | collective-permute-start | bytes 4718600 | tf_op jit(solution)/shard_map/ppermute | solution.py:13
  14.0 4.0 %collective-permute-start.1 = (f32[12,2,128,128]{3,2,1,0:T(8,128)}, f32[12,2,128,128]{3,2,1,0:T(8,128)}, u32[]{:S(2)}, u32[]{:S(2)}) collective-permute-start(f32[12,2,128,128]{3,2,1,0:T(8,128)} %param.21), channel_id=1, source_target_pairs={{0,8},{8,16},{16,24},{24,32},{32,40},{40,48},{48,56},{56,64},{64,7... | collective-permute-start | bytes 4718600 | tf_op jit(solution)/shard_map/ppermute | solution.py:13
  18.0 7.6 %collective-permute-start.2 = (f32[12,2,128,128]{3,2,1,0:T(8,128)}, f32[12,2,128,128]{3,2,1,0:T(8,128)}, u32[]{:S(2)}, u32[]{:S(2)}) collective-permute-start(f32[12,2,128,128]{3,2,1,0:T(8,128)} %param.21), channel_id=1, source_target_pairs={{0,504},{8,0},{16,8},{24,16},{32,24},{40,32},{48,40},{56,48},{64,5... | collective-permute-start | bytes 4718600 | tf_op jit(solution)/shard_map/ppermute | solution.py:13
  25.7 4.3 %collective-permute-start.3 = (f32[12,2,128,128]{3,2,1,0:T(8,128)}, f32[12,2,128,128]{3,2,1,0:T(8,128)}, u32[]{:S(2)}, u32[]{:S(2)}) collective-permute-start(f32[12,2,128,128]{3,2,1,0:T(8,128)} %param.21), channel_id=1, source_target_pairs={{0,496},{8,504},{16,0},{24,8},{32,16},{40,24},{48,32},{56,40},{64,... | collective-permute-start | bytes 4718600 | tf_op jit(solution)/shard_map/ppermute | solution.py:13
  30.0 0.7 fusion.79
  30.7 1.2 reduce_window_sum.17
  31.9 1.2 reduce_window_sum.18
  33.1 0.1 slice.83
  33.2 0.1 copy.89
  33.3 0.1 copy.81
  33.5 0.1 copy.88
  33.6 0.1 copy.72
  33.7 1.2 fusion.26
  34.9 1.1 convert_multiply_fusion
  36.1 0.1 iota_compare_fusion.1
  36.1 1.2 fusion.24
  37.3 1.2 fusion.25
  38.6 0.1 fusion.78
  38.7 1.0 broadcast_multiply_fusion.1
  39.7 1.0 broadcast_multiply_fusion
  40.7 1.5 convolution_multiply_fusion.1
  42.3 1.5 fusion.9
  43.8 1.5 fusion.4
  45.3 0.2 copy.75
  45.5 1.2 copy.76
  46.7 2.0 copy.67
  48.8 1.2 copy.68
  50.0 80.1 %custom-call.4 = f32[4,2,1,128,128]{3,4,2,1,0:T(8,128)} custom-call(f32[4,2,1,128,128]{4,3,2,1,0:T(8,128)} %fusion.9), custom_call_target="InvertDiagBlocksLowerTriangular" | custom-call | tf_op jit(solution)/shard_map/triangular_solve/custom-call.1 | solution.py:45
  130.1 0.1 copy.71
  130.2 80.0 %custom-call.5 = f32[4,2,1,128,128]{3,4,2,1,0:T(8,128)} custom-call(f32[4,2,1,128,128]{4,3,2,1,0:T(8,128)} %fusion.4), custom_call_target="InvertDiagBlocksLowerTriangular" | custom-call | tf_op jit(solution)/shard_map/triangular_solve/custom-call.1 | solution.py:45
  210.2 1.5 convolution_multiply_fusion.4
  211.8 0.3 slice_multiply_fusion
  212.1 2.2 fusion.10
  214.4 2.0 fusion.14
  216.4 2.7 constant_dynamic-update-slice_fusion.4
  219.1 2.7 constant_dynamic-update-slice_fusion.3
  221.8 1.3 constant_dynamic-update-slice_fusion.2
  223.1 2.7 constant_dynamic-update-slice_fusion.1
  225.8 2.7 constant_dynamic-update-slice_fusion
  228.5 3.8 %gather_fusion = f32[4,2,128,128]{3,2,1,0:T(8,128)S(1)} fusion(f32[60,2,128,128]{3,2,1,0:T(8,128)} %constant_dynamic-update-slice_fusion, s32[1024]{0:T(1024)S(1)} %pad_clamp_fusion), kind=kCustom, calls=%fused_computation | custom fusion | bytes 1048592 | tf_op jit(solution)/shard_map/jit(_take)/gather | solution.py:107
  232.4 0.7 convolution_subtract_fusion.1
  233.1 1.2 multiply_add_fusion
  234.3 0.6 convolution_multiply_fusion.2
  235.0 1.9 convolution_subtract_fusion
  236.9 0.7 convolution_multiply_fusion.5
  237.6 0.4 convolution_add_fusion.2
  238.0 0.4 convolution_add_fusion.1
  238.4 0.4 multiply_reduce_fusion
  238.8 0.4 fusion.34
  239.2 0.2 copy.77
  239.4 3.2 %convolution_convert_fusion = bf16[4,256,2048]{2,1,0:T(8,128)(2,1)} fusion(bf16[4,256,256]{1,2,0:T(8,128)(2,1)S(1)} %bitcast.58, bf16[256,2048]{1,0:T(8,128)(2,1)S(1)} %copy-done), kind=kOutput, calls=%fused_computation.1 | convolution fusion | flops 1075838976 | bytes 5767168 | tf_op jit(solution)/shard_map/dot_general | solution.py:134
  242.7 0.1 copy.80
  242.8 0.1 fusion.59
  242.9 1.2 convolution_add_fusion
  244.1 1.3 select_reduce_fusion.4
  245.5 1.9 collective-permute-start.7
  247.4 2.2 collective-permute-start.6
  249.6 6.4 %collective-permute-start.5 = (bf16[4,2,128,128]{3,2,1,0:T(8,128)(2,1)S(1)}, bf16[4,2,128,128]{3,2,1,0:T(8,128)(2,1)S(1)}, u32[]{:S(2)}, u32[]{:S(2)}) collective-permute-start(bf16[4,2,128,128]{3,2,1,0:T(8,128)(2,1)S(1)} %get-tuple-element.4), channel_id=1, source_target_pairs={{0,504},{8,0},{16,8},{24,16},{32,24},{40,32},{48,40},{56,48},{64,5... | collective-permute-start | bytes 786440 | tf_op jit(solution)/shard_map/ppermute | solution.py:13
  256.0 4.3 %collective-permute-start.4 = (bf16[4,2,128,128]{3,2,1,0:T(8,128)(2,1)S(1)}, bf16[4,2,128,128]{3,2,1,0:T(8,128)(2,1)S(1)}, u32[]{:S(2)}, u32[]{:S(2)}) collective-permute-start(bf16[4,2,128,128]{3,2,1,0:T(8,128)(2,1)S(1)} %get-tuple-element.3), channel_id=1, source_target_pairs={{0,496},{8,504},{16,0},{24,8},{32,16},{40,24},{48,32},{56,40},{64,... | collective-permute-start | bytes 786440 | tf_op jit(solution)/shard_map/ppermute | solution.py:13
  260.3 1.1 collective-permute-done.7
  261.4 6.8 %collective-permute-done.6 = bf16[4,2,128,128]{3,2,1,0:T(8,128)(2,1)S(1)} collective-permute-done((bf16[4,2,128,128]{3,2,1,0:T(8,128)(2,1)S(1)}, bf16[4,2,128,128]{3,2,1,0:T(8,128)(2,1)S(1)}, u32[]{:S(2)}, u32[]{:S(2)}) %collective-permute-start.6) | collective-permute-done | bytes 262176 | tf_op jit(solution)/shard_map/ppermute | solution.py:13
  268.1 1.7 collective-permute-done.4
  269.9 0.9 convert_add_fusion
  270.8 10.4 %reduce-scatter.2.cloned.1.call-done = bf16[4,256,256]{2,1,0:T(8,128)(2,1)} async-done(((bf16[4,256,2048]{2,1,0:T(8,128)(2,1)}), bf16[4,256,256]{2,1,0:T(8,128)(2,1)}) %reduce-scatter.2.cloned.1.call-update) | async-done | bytes 524304 | tf_op jit(solution)/shard_map/reduce_scatter | solution.py:137
  (56 shorter events, 0.4 us)
Async XLA Ops:
  7.2 232.3 %copy-start = (bf16[256,2048]{1,0:T(8,128)(2,1)S(1)}, bf16[256,2048]{1,0:T(8,128)(2,1)}, u32[]{:S(2)}) copy-start(bf16[256,2048]{1,0:T(8,128)(2,1)} %param.23) | copy-start | bytes 3145732
  7.2 31.4 %copy-start.10 = (f32[4,2,256]{2,1,0:T(2,128)S(1)}, f32[4,2,256]{2,1,0:T(2,128)}, u32[]{:S(2)}) copy-start(f32[4,2,256]{2,1,0:T(2,128)} %param.20) | copy-start | bytes 24580
  7.2 35.0 %copy-start.11 = (s32[4]{0:T(128)S(1)}, s32[4]{0:T(128)}, u32[]{:S(2)}) copy-start(s32[4]{0:T(128)} %param.25) | copy-start | bytes 52
  7.2 35.0 %copy-start.12 = (s32[4]{0:T(128)S(1)}, s32[4]{0:T(128)}, u32[]{:S(2)}) copy-start(s32[4]{0:T(128)} %param.24) | copy-start | bytes 52
  7.2 274.0 %reduce-scatter.2.cloned.1.call-start = ((), (), s32[]{:S(2)}) async-start(), calls=%async_computation.1 | async-start | bytes 4718592 | tf_op jit(solution)/shard_map/reduce_scatter | solution.py:137
  7.3 209.1 %collective-permute-start = (f32[12,2,128,128]{3,2,1,0:T(8,128)}, f32[12,2,128,128]{3,2,1,0:T(8,128)}, u32[]{:S(2)}, u32[]{:S(2)}) collective-permute-start(f32[12,2,128,128]{3,2,1,0:T(8,128)} %param.21), channel_id=1, source_target_pairs={{0,16},{8,24},{16,32},{24,40},{32,48},{40,56},{48,64},{56,72},{64,... | collective-permute-start | bytes 4718600 | tf_op jit(solution)/shard_map/ppermute | solution.py:13
  14.0 205.1 %collective-permute-start.1 = (f32[12,2,128,128]{3,2,1,0:T(8,128)}, f32[12,2,128,128]{3,2,1,0:T(8,128)}, u32[]{:S(2)}, u32[]{:S(2)}) collective-permute-start(f32[12,2,128,128]{3,2,1,0:T(8,128)} %param.21), channel_id=1, source_target_pairs={{0,8},{8,16},{16,24},{24,32},{32,40},{40,48},{48,56},{56,64},{64,7... | collective-permute-start | bytes 4718600 | tf_op jit(solution)/shard_map/ppermute | solution.py:13
  18.0 205.1 %collective-permute-start.2 = (f32[12,2,128,128]{3,2,1,0:T(8,128)}, f32[12,2,128,128]{3,2,1,0:T(8,128)}, u32[]{:S(2)}, u32[]{:S(2)}) collective-permute-start(f32[12,2,128,128]{3,2,1,0:T(8,128)} %param.21), channel_id=1, source_target_pairs={{0,504},{8,0},{16,8},{24,16},{32,24},{40,32},{48,40},{56,48},{64,5... | collective-permute-start | bytes 4718600 | tf_op jit(solution)/shard_map/ppermute | solution.py:13
  25.7 200.2 %collective-permute-start.3 = (f32[12,2,128,128]{3,2,1,0:T(8,128)}, f32[12,2,128,128]{3,2,1,0:T(8,128)}, u32[]{:S(2)}, u32[]{:S(2)}) collective-permute-start(f32[12,2,128,128]{3,2,1,0:T(8,128)} %param.21), channel_id=1, source_target_pairs={{0,496},{8,504},{16,0},{24,8},{32,16},{40,24},{48,32},{56,40},{64,... | collective-permute-start | bytes 4718600 | tf_op jit(solution)/shard_map/ppermute | solution.py:13
  37.3 8.0 %copy-start.9 = (bf16[4,256,256]{2,1,0:T(8,128)(2,1)S(1)}, bf16[4,256,256]{2,1,0:T(8,128)(2,1)}, u32[]{:S(2)}) copy-start(bf16[4,256,256]{2,1,0:T(8,128)(2,1)} %param.18) | copy-start | bytes 1572868
  38.6 171.6 %copy-start.2 = (f32[4,128,128]{2,1,0:T(8,128)}, f32[4,128,128]{2,1,0:T(8,128)S(1)}, u32[]{:S(2)}) copy-start(f32[4,128,128]{2,1,0:T(8,128)S(1)} %get-tuple-element.14) | copy-start | bytes 786436
  43.8 167.9 %copy-start.15 = (s32[4]{0:T(128)S(1)}, s32[4]{0:T(128)}, u32[]{:S(2)}) copy-start(s32[4]{0:T(128)} %param.26) | copy-start | bytes 52
  210.2 4.1 %copy-start.4 = (f32[4,2,128,128]{3,2,1,0:T(8,128)S(1)}, f32[4,2,128,128]{3,2,1,0:T(8,128)}, u32[]{:S(2)}) copy-start(f32[4,2,128,128]{3,2,1,0:T(8,128)} %broadcast_multiply_fusion) | copy-start | bytes 1572868
  210.2 4.1 %copy-start.8 = (f32[4,2,1,128,128]{3,4,2,1,0:T(8,128)S(1)}, f32[4,2,1,128,128]{3,4,2,1,0:T(8,128)}, u32[]{:S(2)}) copy-start(f32[4,2,1,128,128]{3,4,2,1,0:T(8,128)} %custom-call.5) | copy-start | bytes 1572868
  214.4 7.5 %copy-start.7 = (f32[12,2,128,128]{3,2,1,0:T(8,128)S(1)}, f32[12,2,128,128]{3,2,1,0:T(8,128)}, u32[]{:S(2)}) copy-start(f32[12,2,128,128]{3,2,1,0:T(8,128)} %param.21) | copy-start | bytes 4718596
  232.4 4.5 %copy-start.3 = (f32[4,128,128]{2,1,0:T(8,128)S(1)}, f32[4,128,128]{2,1,0:T(8,128)}, u32[]{:S(2)}) copy-start(f32[4,128,128]{2,1,0:T(8,128)} %copy-done.2) | copy-start | bytes 786436
  232.4 5.2 %copy-start.6 = (f32[4,2,128,128]{3,2,1,0:T(8,128)S(1)}, f32[4,2,128,128]{3,2,1,0:T(8,128)}, u32[]{:S(2)}) copy-start(f32[4,2,128,128]{3,2,1,0:T(8,128)} %convolution_multiply_fusion.4) | copy-start | bytes 1572868
  233.1 4.9 %copy-start.5 = (f32[4,2,128,128]{3,2,1,0:T(8,128)S(1)}, f32[4,2,128,128]{3,2,1,0:T(8,128)}, u32[]{:S(2)}) copy-start(f32[4,2,128,128]{3,2,1,0:T(8,128)} %convolution_multiply_fusion.1) | copy-start | bytes 1572868
  234.9 3.9 %copy-start.1 = (f32[4,256,2,128]{3,1,2,0:T(8,128)S(1)}, f32[4,256,2,128]{3,1,2,0:T(8,128)}, u32[]{:S(2)}) copy-start(f32[4,256,2,128]{3,1,2,0:T(8,128)} %copy.76) | copy-start | bytes 3145732
  234.9 3.9 %copy-start.14 = (f32[128]{0:T(128)S(1)}, f32[128]{0:T(128)}, u32[]{:S(2)}) copy-start(f32[128]{0:T(128)} %param.22) | copy-start | bytes 1540
  239.4 3.4 %copy-start.13 = (s32[4]{0:T(128)S(1)}, s32[4]{0:T(128)}, u32[]{:S(2)}) copy-start(s32[4]{0:T(128)} %param.27) | copy-start | bytes 52
  245.5 15.9 %collective-permute-start.7 = (bf16[4,2,128,128]{3,2,1,0:T(8,128)(2,1)S(1)}, bf16[4,2,128,128]{3,2,1,0:T(8,128)(2,1)S(1)}, u32[]{:S(2)}, u32[]{:S(2)}) collective-permute-start(bf16[4,2,128,128]{3,2,1,0:T(8,128)(2,1)S(1)} %get-tuple-element.7), channel_id=1, source_target_pairs={{0,16},{8,24},{16,32},{24,40},{32,48},{40,56},{48,64},{56,72},{64,... | collective-permute-start | bytes 786440 | tf_op jit(solution)/shard_map/ppermute | solution.py:13
  247.4 20.7 %collective-permute-start.6 = (bf16[4,2,128,128]{3,2,1,0:T(8,128)(2,1)S(1)}, bf16[4,2,128,128]{3,2,1,0:T(8,128)(2,1)S(1)}, u32[]{:S(2)}, u32[]{:S(2)}) collective-permute-start(bf16[4,2,128,128]{3,2,1,0:T(8,128)(2,1)S(1)} %get-tuple-element.6), channel_id=1, source_target_pairs={{0,8},{8,16},{16,24},{24,32},{32,40},{40,48},{48,56},{56,64},{64,7... | collective-permute-start | bytes 786440 | tf_op jit(solution)/shard_map/ppermute | solution.py:13
  249.6 18.5 %collective-permute-start.5 = (bf16[4,2,128,128]{3,2,1,0:T(8,128)(2,1)S(1)}, bf16[4,2,128,128]{3,2,1,0:T(8,128)(2,1)S(1)}, u32[]{:S(2)}, u32[]{:S(2)}) collective-permute-start(bf16[4,2,128,128]{3,2,1,0:T(8,128)(2,1)S(1)} %get-tuple-element.4), channel_id=1, source_target_pairs={{0,504},{8,0},{16,8},{24,16},{32,24},{40,32},{48,40},{56,48},{64,5... | collective-permute-start | bytes 786440 | tf_op jit(solution)/shard_map/ppermute | solution.py:13
  256.0 13.9 %collective-permute-start.4 = (bf16[4,2,128,128]{3,2,1,0:T(8,128)(2,1)S(1)}, bf16[4,2,128,128]{3,2,1,0:T(8,128)(2,1)S(1)}, u32[]{:S(2)}, u32[]{:S(2)}) collective-permute-start(bf16[4,2,128,128]{3,2,1,0:T(8,128)(2,1)S(1)} %get-tuple-element.3), channel_id=1, source_target_pairs={{0,496},{8,504},{16,0},{24,8},{32,16},{40,24},{48,32},{56,40},{64,... | collective-permute-start | bytes 786440 | tf_op jit(solution)/shard_map/ppermute | solution.py:13
Sparse Core Ops, SparseCore 0:
  242.8 38.3 reduce-scatter.1
where the time goes:
time: 290 us; the launch traced here: 288 us
  other arithmetic  173 us (60%)
  starting transfers between devices  37.5 us (13%)
  local copies, waits for them, and re-layouts  22.4 us (8%)
  matrix products  20.7 us (7%)
  waiting for transfers between devices  20 us (7%)
  between operations  14.5 us (5%)
    another operation x5, other arithmetic, delta_block(): lax.linalg.triangular_solve(system, stacked, left_side=True, lower=True,...  160 us
    ppermute x8, starting transfers between devices, shifted(): lax.ppermute(x, axis, [(i, (i + by) % devices) for i in range(devices)])  37.4 us
    unnamed x40, local copies, waits for them, and re-layouts  11.9 us
    reduce_scatter x1, waiting for transfers between devices, on_device(): lax.psum_scatter(partial_value.astype(jnp.bfloat16), 'tensor', scatter_di...  10.4 us
    ppermute x8, waiting for transfers between devices, shifted(): lax.ppermute(x, axis, [(i, (i + by) % devices) for i in range(devices)])  9.61 us
    dot_general x6, matrix products, block_dot(): jnp.einsum(equation, first_operand, second_operand, precision=lax.Precisi...  6.84 us
    dot_general x6, matrix products, exact_dot(): jnp.einsum(equation, first_operand, second_operand, precision=lax.Precisi...  6.33 us
  transfers between devices with their start and end apart: 9, of which 4 were waited for; matrix products, arithmetic and copies ran while one was open for 69% of the time, Pallas kernels for 0%

commit v1 on v0

v1 whole, which is shorter than its diff:
```python
import jax
import jax.numpy as jnp
from jax import lax
from jax.experimental import pallas as pl
from jax.experimental.pallas import tpu as pltpu
from jax.sharding import PartitionSpec as P

DK = 128
DV = 128
REACH = 2
SMALL = 8

def split(x):
    hi = x.astype(jnp.bfloat16)
    return hi, (x - hi.astype(jnp.float32)).astype(jnp.bfloat16)


def dot1(a, b):
    return jnp.dot(a, b, preferred_element_type=jnp.float32)


def dot3(a, b):
    (a_hi, a_lo), (b_hi, b_lo) = a, b
    return dot1(a_hi, b_hi) + (dot1(a_lo, b_hi) + dot1(a_hi, b_lo))


def dot_nt(a, b):
    return lax.dot_general(a, b, (((1,), (1,)), ((), ())), preferred_element_type=jnp.float32)


def dot_tn(a, b):
    return lax.dot_general(a, b, (((0,), (0,)), ((), ())), preferred_element_type=jnp.float32)


def iota(shape, dim):
    return lax.broadcasted_iota(jnp.int32, shape, dim)


def solve_small(compact):
    rows, lanes = compact.shape
    place = iota((rows, lanes), 1) % SMALL
    inverse = jnp.where(place == iota((rows, lanes), 0) % SMALL, 1.0, 0.0)
    for j in range(SMALL - 1):
        column = jnp.where(place == j, compact, 0.0)
        if j:
            column = pltpu.roll(column, lanes - j, 1)
        for step in (1, 2, 4):
            column = column + pltpu.roll(column, step, 1)
        groups = inverse.reshape(rows // SMALL, SMALL, lanes)
        row = jnp.broadcast_to(groups[:, j : j + 1, :], groups.shape).reshape(rows, lanes)
        inverse = inverse - column * row
    return inverse


def invert_unit_lower(systems):
    n = systems[0].shape[0]
    half = n // 2
    block_of_lane = iota((n // SMALL, SMALL, n), 2) // SMALL
    own = block_of_lane == iota((n // SMALL, SMALL, n), 0)
    parts = []
    for system in systems:
        compact = jnp.sum(
            jnp.where(own, system.reshape(n // SMALL, SMALL, n), 0.0), axis=0
        )
        parts += [compact[:, :half], compact[:, half:]]
    small = solve_small(jnp.concatenate(parts, axis=0))
    inverses = []
    for i in range(len(systems)):
        left = small[2 * i * SMALL : (2 * i + 1) * SMALL]
        right = small[(2 * i + 1) * SMALL : (2 * i + 2) * SMALL]
        wide = jnp.concatenate([left, right], axis=1)
        inverses.append(
            jnp.where(own, jnp.broadcast_to(wide[None], own.shape), 0.0).reshape(n, n)
        )
    size = SMALL
    while size < half:
        pairs = n // (2 * size)
        even = iota((pairs, size, n), 2) // size == 2 * iota((pairs, size, n), 0)
        grown = []
        for system, inverse in zip(systems, inverses):
            below = jnp.where(even, system.reshape(pairs, 2, size, n)[:, 1], 0.0)
            folded = inverse.reshape(pairs, 2, size, n)
            lower = folded[:, 1].reshape(half, n)
            inner = dot3(split(below.reshape(half, n)), split(inverse))
            spread = jnp.stack(
                [jnp.zeros((pairs, size, n), jnp.float32), inner.reshape(pairs, size, n)], axis=1
            ).reshape(n, n)
            lower = lower - dot3(split(lower), split(spread))
            grown.append(
                jnp.stack([folded[:, 0], lower.reshape(pairs, size, n)], axis=1).reshape(n, n)
            )
        inverses = grown
        size *= 2
    done = []
    for system, inverse in zip(systems, inverses):
        top, bottom = inverse[:half, :half], inverse[half:, half:]
        cross = dot3(split(system[half:, :half]), split(top))
        cross = -dot3(split(bottom), split(cross))
        done.append(
            jnp.concatenate(
                [
                    jnp.concatenate([top, jnp.zeros_like(top)], axis=1),
                    jnp.concatenate([cross, bottom], axis=1),
                ],
                axis=0,
            )
        )
    return done


def prepare(r, q_ref, k_ref, v_ref, gate_ref, decay_ref, rate_ref, gain_ref, zhi_ref, zlo_ref, base_ref, gain_gate_ref):
    tokens = q_ref.shape[1]
    heads = decay_ref.shape[1]
    q, k = q_ref[r], k_ref[r]
    qf, kf = q.astype(jnp.float32), k.astype(jnp.float32)
    rq = lax.rsqrt(jnp.sum(qf * qf, axis=1, keepdims=True) + 1e-06) * DK ** (-0.5)
    k_square = jnp.sum(kf * kf, axis=1, keepdims=True)
    rk = lax.rsqrt(k_square + 1e-06)
    row, lane = iota((tokens, tokens), 0), iota((tokens, tokens), 1)
    raw_kk = dot_nt(k, k)
    raw_qk = dot_nt(q, k)
    rk_lane = lax.rsqrt(jnp.sum(jnp.where(row == lane, raw_kk, 0.0), axis=0, keepdims=True) + 1e-06)
    decay = decay_ref[r]
    hi, rest = split(decay)
    rest = decay - hi.astype(jnp.float32)
    mid, low = split(rest)
    upto = jnp.where(row <= lane, 1.0, 0.0).astype(jnp.bfloat16)
    running = dot1(low, upto) + dot1(mid, upto) + dot1(hi, upto)
    columns = jnp.concatenate(
        [running, rate_ref[r], jnp.zeros((8 - 2 * heads, tokens), jnp.float32)], axis=0
    ).T
    systems, reads = [], []
    for h in range(heads):
        spread = jnp.where(row >= lane, columns[:, h : h + 1] - running[h : h + 1], -jnp.inf)
        within = jnp.exp(spread) * rk_lane
        rate = columns[:, heads + h : heads + h + 1]
        systems.append(jnp.where(row > lane, (rate * rk) * (within * raw_kk), 0.0))
        reads.append(rq * (within * raw_qk))
    inverses = invert_unit_lower(systems)
    for h in range(heads):
        slot = r * heads + h
        g = columns[:, h : h + 1]
        rate = columns[:, heads + h : heads + h + 1]
        from_start = jnp.exp(g)
        values = v_ref[r, :, h * DV : (h + 1) * DV].astype(jnp.float32)
        right = jnp.concatenate([rate * values, (rate * from_start * rk) * kf], axis=1)
        solved = split(dot3(split(inverses[h]), split(right)))
        last = columns[tokens - 1 : tokens, h : h + 1]
        to_end = (jnp.exp(last - g) * rk) * kf
        read = dot3(split(reads[h]), solved)
        end_hi, end_lo = split(to_end)
        end = dot_tn(end_hi, solved[0]) + (dot_tn(end_lo, solved[0]) + dot_tn(end_hi, solved[1]))
        base_ref[slot, :tokens] = read[:, :DV]
        base_ref[slot, tokens:] = end[:, :DV]
        from_state = (from_start * rq) * qf - read[:, DV:]
        eye = iota((DK, DK), 0) == iota((DK, DK), 1)
        to_state = jnp.where(eye, jnp.exp(last), 0.0) - end[:, DV:]
        z_hi, z_lo = split(jnp.concatenate([from_state, to_state], axis=0))
        zhi_ref[slot] = z_hi
        zlo_ref[slot] = z_lo
        gate = gate_ref[r, :, h * DV : (h + 1) * DV].astype(jnp.float32)
        gain_gate_ref[slot] = gain_ref[...] * (gate / (1.0 + jnp.exp(-gate)))


def finish(slot, start, zhi_ref, zlo_ref, base_ref, gain_gate_ref):
    tokens = gain_gate_ref.shape[1]
    whole = dot1(zhi_ref[slot], start) + dot1(zlo_ref[slot], start) + base_ref[slot]
    attended, end = whole[:tokens], whole[tokens:]
    scale = lax.rsqrt(jnp.mean(attended * attended, axis=1, keepdims=True) + 1e-06)
    return (attended * scale * gain_gate_ref[slot]).astype(jnp.bfloat16), end


def delta_kernel(q_ref, k_ref, v_ref, gate_ref, decay_ref, rate_ref, gain_ref, start_ref, normed_ref, end_ref, zhi_ref, zlo_ref, base_ref, gain_gate_ref):
    heads = decay_ref.shape[1]

    @pl.loop(0, q_ref.shape[0])
    def _(r):
        prepare(r, q_ref, k_ref, v_ref, gate_ref, decay_ref, rate_ref, gain_ref, zhi_ref, zlo_ref, base_ref, gain_gate_ref)

    @pl.loop(0, q_ref.shape[0])
    def _(r):
        for h in range(heads):
            normed, end = finish(
                r * heads + h, start_ref[r, h].astype(jnp.bfloat16), zhi_ref, zlo_ref, base_ref, gain_gate_ref
            )
            normed_ref[r, :, h * DV : (h + 1) * DV] = normed
            end_ref[r, h] = end


def delta(q, k, v, gate, decay, rate, gain, start):
    requests, tokens = q.shape[:2]
    heads = decay.shape[1]
    return pl.pallas_call(
        delta_kernel,
        out_shape=(
            jax.ShapeDtypeStruct(v.shape, jnp.bfloat16),
            jax.ShapeDtypeStruct(start.shape, jnp.float32),
        ),
        scratch_shapes=[
            pltpu.VMEM((requests * heads, tokens + DK, DK), jnp.bfloat16),
            pltpu.VMEM((requests * heads, tokens + DK, DK), jnp.bfloat16),
            pltpu.VMEM((requests * heads, tokens + DK, DV), jnp.float32),
            pltpu.VMEM((requests * heads, tokens, DV), jnp.float32),
        ],
        compiler_params=pltpu.CompilerParams(vmem_limit_bytes=48 * 1024 * 1024),
        name="delta",
    )(q, k, v, gate, decay, rate, gain, start)


def shifted(x, axis, by):
    devices = lax.axis_size(axis)
    return lax.ppermute(x, axis, [(i, (i + by) % devices) for i in range(devices)])


def on_device(
    queries,
    key_heads,
    values_in,
    out_gate,
    log_decay,
    write_rate,
    cache_states,
    norm_gain,
    out_proj,
    hit_owner,
    hit_node,
    prefix_len,
    write_slot,
):
    requests_here, length = queries.shape[:2]
    head_count = log_decay.shape[1]
    slot_count = cache_states.shape[0]
    workers = lax.axis_size("worker")
    worker_id = lax.axis_index("worker")
    cached = prefix_len > 0
    relative = (hit_owner - worker_id + workers + REACH) % workers - REACH
    pieces = []
    for offset in range(-REACH, REACH + 1):
        if offset == 0:
            pieces.append(cache_states)
        else:
            pieces.append(shifted(cache_states, "worker", -offset))
    window = jnp.concatenate(pieces, axis=0)
    start_state = jnp.take(window, (relative + REACH) * slot_count + hit_node, axis=0)
    start_state = jnp.where(cached[:, None, None, None], start_state, 0.0)
    normed, running_state = delta(
        queries, key_heads, values_in, out_gate, log_decay, write_rate, norm_gain[None], start_state
    )
    partial_value = jnp.dot(
        normed.reshape(requests_here * length, head_count * DV), out_proj, preferred_element_type=jnp.float32
    ).reshape(requests_here, length, out_proj.shape[1])
    mixed = lax.psum_scatter(
        partial_value.astype(jnp.bfloat16), "tensor", scatter_dimension=2, tiled=True
    )
    target_worker = write_slot // requests_here
    target_lane = write_slot % requests_here
    target_move = (target_worker - worker_id + workers + REACH) % workers - REACH
    lane_ids = jnp.arange(requests_here, dtype=jnp.int32)
    end_states = jnp.zeros_like(running_state)
    for offset in range(-REACH, REACH + 1):
        routed = (target_move == offset)[:, None] & (target_lane[:, None] == lane_ids[None, :])
        packed = jnp.sum(
            jnp.where(routed[:, :, None, None, None], running_state[:, None], 0.0), axis=0
        )
        if offset != 0:
            packed = shifted(packed.astype(jnp.bfloat16), "worker", offset).astype(packed.dtype)
        end_states = end_states + packed
    return (mixed, end_states)


def solution(mesh):
    in_specs = (
        P("worker", None, "tensor"),
        P("worker", None, "tensor"),
        P("worker", None, "tensor"),
        P("worker", None, "tensor"),
        P("worker", "tensor", None),
        P("worker", "tensor", None),
        P("worker", "tensor", None, None),
        P(),
        P("tensor", None),
        P("worker"),
        P("worker"),
        P("worker"),
        P("worker"),
    )
    out_specs = (P("worker", None, "tensor"), P("worker", "tensor", None, None))
    return jax.shard_map(
        on_device, mesh=mesh, in_specs=in_specs, out_specs=out_specs, check_vma=False
    )
```

time: 290 us -> 207 us (0.71)
  other arithmetic: 173 us -> 3.88 us
  waiting for transfers between devices: 20 us -> 111 us
  Pallas kernels: 0 us -> 19.2 us
  matrix products: 20.7 us -> 3.21 us
  local copies, waits for them, and re-layouts: 22.4 us -> 16.1 us
    another operation x7 -> x0, other arithmetic: 163 us -> none  [the longest x5 160 us: delta_block(): lax.linalg.triangular_solve(system, stacked, left_side=True, lower=True,...]
    ppermute x8, waiting for transfers between devices: 9.61 us -> 101 us  [shifted(): lax.ppermute(x, axis, [(i, (i + by) % devices) for i in range(devices)])]
    pallas_call x0 -> x1, Pallas kernels: none -> 19.2 us  [delta(): pl.pallas_call(delta_kernel, out_shape=(jax.ShapeDtypeStruct(v.shape, jnp...]
    dot_general x13 -> x1, matrix products: 16.4 us -> 3.21 us  [on_device(): jnp.dot(normed.reshape(requests_here * length, head_count * DV), out_proj...]
    mul x5 -> x0, other arithmetic: 4.71 us -> none  [the longest x2 2.01 us: delta_block(): (rate_blk * from_start)[..., None] * key_blk]
    another operation x2 -> x0, matrix products: 4.26 us -> none  [delta_block(): lax.linalg.triangular_solve(system, stacked, left_side=True, lower=True,...]
    unnamed x40 -> x24, local copies, waits for them, and re-layouts: 11.9 us -> 9.56 us
  transfers between devices with their start and end apart: 9 -> 9, of which waited for: 4 -> 6; matrix products, arithmetic and copies ran while one was open for 69% -> 6% of each run, Pallas kernels for 0% -> 0%
where the time goes in v1:
time: 207 us; the launch traced here: 205 us
  waiting for transfers between devices  111 us (54%)
  starting transfers between devices  37.5 us (18%)
  Pallas kernels  19.2 us (9%)
  local copies, waits for them, and re-layouts  16.1 us (8%)
  between operations  14.3 us (7%)
  other arithmetic  3.88 us (2%)
  matrix products  3.21 us (2%)
    ppermute x8, waiting for transfers between devices, shifted(): lax.ppermute(x, axis, [(i, (i + by) % devices) for i in range(devices)])  101 us
    ppermute x8, starting transfers between devices, shifted(): lax.ppermute(x, axis, [(i, (i + by) % devices) for i in range(devices)])  37.4 us
    pallas_call x1, Pallas kernels, delta(): pl.pallas_call(delta_kernel, out_shape=(jax.ShapeDtypeStruct(v.shape, jnp...  19.2 us
    reduce_scatter x1, waiting for transfers between devices, on_device(): lax.psum_scatter(partial_value.astype(jnp.bfloat16), 'tensor', scatter_di...  10.5 us
    unnamed x24, local copies, waits for them, and re-layouts  9.56 us
  transfers between devices with their start and end apart: 9, of which 6 were waited for; matrix products, arithmetic and copies ran while one was open for 6% of the time, Pallas kernels for 0%

profile of v1, /device:TPU:1, one launch (start us, length us, event | category | flops | bytes accessed | tf_op | source)
XLA Modules:
  0.0 205.5 jit_solution(14162847258052111311)
XLA Ops:
  7.2 0.0 copy-start
  7.2 0.0 copy-start.8
  7.2 0.0 reduce-scatter.2.cloned.1.call-start
  7.2 6.8 %collective-permute-start = (f32[12,2,128,128]{3,2,1,0:T(8,128)}, f32[12,2,128,128]{3,2,1,0:T(8,128)}, u32[]{:S(2)}, u32[]{:S(2)}) collective-permute-start(f32[12,2,128,128]{3,2,1,0:T(8,128)} %param.19), channel_id=1, source_target_pairs={{0,16},{8,24},{16,32},{24,40},{32,48},{40,56},{48,64},{56,72},{64,... | collective-permute-start | bytes 4718600 | tf_op jit(solution)/shard_map/ppermute | solution.py:212
  14.0 4.0 %collective-permute-start.1 = (f32[12,2,128,128]{3,2,1,0:T(8,128)}, f32[12,2,128,128]{3,2,1,0:T(8,128)}, u32[]{:S(2)}, u32[]{:S(2)}) collective-permute-start(f32[12,2,128,128]{3,2,1,0:T(8,128)} %param.19), channel_id=1, source_target_pairs={{0,8},{8,16},{16,24},{24,32},{32,40},{40,48},{48,56},{56,64},{64,7... | collective-permute-start | bytes 4718600 | tf_op jit(solution)/shard_map/ppermute | solution.py:212
  18.0 7.6 %collective-permute-start.2 = (f32[12,2,128,128]{3,2,1,0:T(8,128)}, f32[12,2,128,128]{3,2,1,0:T(8,128)}, u32[]{:S(2)}, u32[]{:S(2)}) collective-permute-start(f32[12,2,128,128]{3,2,1,0:T(8,128)} %param.19), channel_id=1, source_target_pairs={{0,504},{8,0},{16,8},{24,16},{32,24},{40,32},{48,40},{56,48},{64,5... | collective-permute-start | bytes 4718600 | tf_op jit(solution)/shard_map/ppermute | solution.py:212
  25.6 4.3 %collective-permute-start.3 = (f32[12,2,128,128]{3,2,1,0:T(8,128)}, f32[12,2,128,128]{3,2,1,0:T(8,128)}, u32[]{:S(2)}, u32[]{:S(2)}) collective-permute-start(f32[12,2,128,128]{3,2,1,0:T(8,128)} %param.19), channel_id=1, source_target_pairs={{0,496},{8,504},{16,0},{24,8},{32,16},{40,24},{48,32},{56,40},{64,... | collective-permute-start | bytes 4718600 | tf_op jit(solution)/shard_map/ppermute | solution.py:212
  29.9 0.7 compare_and_fusion
  30.6 0.7 broadcast_compare_fusion.5
  31.3 58.5 %collective-permute-done = f32[12,2,128,128]{3,2,1,0:T(8,128)} collective-permute-done((f32[12,2,128,128]{3,2,1,0:T(8,128)}, f32[12,2,128,128]{3,2,1,0:T(8,128)}, u32[]{:S(2)}, u32[]{:S(2)}) %collective-permute-start) | collective-permute-done | bytes 1572896 | tf_op jit(solution)/shard_map/ppermute | solution.py:212
  89.8 2.7 %constant_dynamic-update-slice_fusion.4 = f32[60,2,128,128]{3,2,1,0:T(8,128)} fusion(f32[12,2,128,128]{3,2,1,0:T(8,128)} %collective-permute-done), kind=kLoop, calls=%fused_computation.14 | loop fusion | bytes 3145728
  92.5 31.1 %collective-permute-done.1 = f32[12,2,128,128]{3,2,1,0:T(8,128)} collective-permute-done((f32[12,2,128,128]{3,2,1,0:T(8,128)}, f32[12,2,128,128]{3,2,1,0:T(8,128)}, u32[]{:S(2)}, u32[]{:S(2)}) %collective-permute-start.1) | collective-permute-done | bytes 1572896 | tf_op jit(solution)/shard_map/ppermute | solution.py:212
  123.5 2.7 %constant_dynamic-update-slice_fusion.3 = f32[60,2,128,128]{3,2,1,0:T(8,128)} fusion(f32[60,2,128,128]{3,2,1,0:T(8,128)} %constant_dynamic-update-slice_fusion.4, f32[12,2,128,128]{3,2,1,0:T(8,128)} %collective-permute-done.1), kind=kLoop, calls=%fused_computation.13 | loop fusion | bytes 3145728
  126.3 0.0 copy-done.8
  126.3 1.3 constant_dynamic-update-slice_fusion.2
  127.5 0.0 copy-start.1
  127.5 0.0 copy-start.2
  127.5 0.0 copy-start.3
  127.5 0.0 copy-start.4
  127.5 0.0 copy-start.5
  127.5 0.0 copy-start.6
  127.6 0.0 copy-start.7
  127.6 0.0 collective-permute-done.2
  127.6 2.8 %constant_dynamic-update-slice_fusion.1 = f32[60,2,128,128]{3,2,1,0:T(8,128)} fusion(f32[60,2,128,128]{3,2,1,0:T(8,128)} %constant_dynamic-update-slice_fusion.2, f32[12,2,128,128]{3,2,1,0:T(8,128)} %collective-permute-done.2), kind=kLoop, calls=%fused_computation.11 | loop fusion | bytes 3145728
  130.4 0.0 collective-permute-done.3
  130.4 2.7 %constant_dynamic-update-slice_fusion = f32[60,2,128,128]{3,2,1,0:T(8,128)} fusion(f32[60,2,128,128]{3,2,1,0:T(8,128)} %constant_dynamic-update-slice_fusion.1, f32[12,2,128,128]{3,2,1,0:T(8,128)} %collective-permute-done.3), kind=kLoop, calls=%fused_computation.10 | loop fusion | bytes 3145728 | tf_op jit(solution)/shard_map/concatenate | solution.py:243
  133.1 3.8 %gather_fusion = f32[4,2,128,128]{3,2,1,0:T(8,128)S(1)} fusion(f32[60,2,128,128]{3,2,1,0:T(8,128)} %constant_dynamic-update-slice_fusion, s32[1024]{0:T(1024)S(1)} %pad_clamp_fusion), kind=kCustom, calls=%fused_computation | custom fusion | bytes 1048592 | tf_op jit(solution)/shard_map/jit(_take)/gather | solution.py:244
  136.9 0.1 select_select_fusion.start_ref
  137.1 0.0 copy-done.1
  137.1 0.0 copy-done.2
  137.1 0.0 copy-done.3
  137.1 0.0 copy-done.4
  137.1 0.0 copy-done.5
  137.1 0.0 copy-done.6
  137.1 0.0 copy-done.7
  137.1 19.2 %delta.1 = (bf16[4,256,256]{2,1,0:T(8,128)(2,1)S(1)}, f32[4,2,128,128]{3,2,1,0:T(8,128)S(1)}) custom-call(bf16[4,256,128]{2,1,0:T(8,128)(2,1)S(1)} %copy-done.3, bf16[4,256,128]{2,1,0:T(8,128)(2,1)S(1)} %copy-done.4, bf16[4,256,256]{2,1,0:T(8,128)(2,1)S(1)} %copy-done.1, bf16[4,256,256]{2,1,0:T(8,128)(2,1)S(1)} %copy-done.2, f32[4,2,256]{2,1,0:T(2,128)S(1)} %copy-done.5, ...), custom_call_target="tpu_custom_call" | custom-call | tf_op jit(solution)/shard_map/delta/pallas_call | solution.py:193
  156.3 0.0 copy-done
  156.3 0.0 copy-start.9
  156.3 3.2 %convolution_convert_fusion = bf16[4,256,2048]{2,1,0:T(8,128)(2,1)} fusion(bf16[4,256,256]{2,1,0:T(8,128)(2,1)S(1)} %get-tuple-element.4, bf16[256,2048]{1,0:T(8,128)(2,1)S(1)} %copy-done), kind=kOutput, calls=%fused_computation.1 | convolution fusion | flops 1075838976 | bytes 5767168 | tf_op jit(solution)/shard_map/dot_general | solution.py:249
  159.6 0.0 reduce-scatter.2.cloned.1.call-update
  159.6 0.0 copy-done.9
  159.6 0.1 fusion.1
  159.7 1.3 select_reduce_fusion.4
  161.1 1.9 collective-permute-start.7
  163.0 1.9 collective-permute-start.6
  164.9 6.7 %collective-permute-start.5 = (bf16[4,2,128,128]{3,2,1,0:T(8,128)(2,1)S(1)}, bf16[4,2,128,128]{3,2,1,0:T(8,128)(2,1)S(1)}, u32[]{:S(2)}, u32[]{:S(2)}) collective-permute-start(bf16[4,2,128,128]{3,2,1,0:T(8,128)(2,1)S(1)} %get-tuple-element.7), channel_id=1, source_target_pairs={{0,504},{8,0},{16,8},{24,16},{32,24},{40,32},{48,40},{56,48},{64,5... | collective-permute-start | bytes 786440 | tf_op jit(solution)/shard_map/ppermute | solution.py:212
  171.6 4.3 %collective-permute-start.4 = (bf16[4,2,128,128]{3,2,1,0:T(8,128)(2,1)S(1)}, bf16[4,2,128,128]{3,2,1,0:T(8,128)(2,1)S(1)}, u32[]{:S(2)}, u32[]{:S(2)}) collective-permute-start(bf16[4,2,128,128]{3,2,1,0:T(8,128)(2,1)S(1)} %get-tuple-element.6), channel_id=1, source_target_pairs={{0,496},{8,504},{16,0},{24,8},{32,16},{40,24},{48,32},{56,40},{64,... | collective-permute-start | bytes 786440 | tf_op jit(solution)/shard_map/ppermute | solution.py:212
  175.9 1.7 collective-permute-done.7
  177.5 4.4 %collective-permute-done.6 = bf16[4,2,128,128]{3,2,1,0:T(8,128)(2,1)S(1)} collective-permute-done((bf16[4,2,128,128]{3,2,1,0:T(8,128)(2,1)S(1)}, bf16[4,2,128,128]{3,2,1,0:T(8,128)(2,1)S(1)}, u32[]{:S(2)}, u32[]{:S(2)}) %collective-permute-start.6) | collective-permute-done | bytes 262176 | tf_op jit(solution)/shard_map/ppermute | solution.py:212
  182.0 0.0 collective-permute-done.5
  182.0 5.2 %collective-permute-done.4 = bf16[4,2,128,128]{3,2,1,0:T(8,128)(2,1)S(1)} collective-permute-done((bf16[4,2,128,128]{3,2,1,0:T(8,128)(2,1)S(1)}, bf16[4,2,128,128]{3,2,1,0:T(8,128)(2,1)S(1)}, u32[]{:S(2)}, u32[]{:S(2)}) %collective-permute-start.4) | collective-permute-done | bytes 262176 | tf_op jit(solution)/shard_map/ppermute | solution.py:212
  187.2 0.9 convert_add_fusion
  188.2 10.5 %reduce-scatter.2.cloned.1.call-done = bf16[4,256,256]{2,1,0:T(8,128)(2,1)} async-done(((bf16[4,256,2048]{2,1,0:T(8,128)(2,1)}), bf16[4,256,256]{2,1,0:T(8,128)(2,1)}) %reduce-scatter.2.cloned.1.call-update) | async-done | bytes 524304 | tf_op jit(solution)/shard_map/reduce_scatter | solution.py:252
  (4 shorter events, 0.0 us)
Async XLA Ops:
  7.2 149.2 %copy-start = (bf16[256,2048]{1,0:T(8,128)(2,1)S(1)}, bf16[256,2048]{1,0:T(8,128)(2,1)}, u32[]{:S(2)}) copy-start(bf16[256,2048]{1,0:T(8,128)(2,1)} %param.21) | copy-start | bytes 3145732
  7.2 119.1 %copy-start.8 = (f32[12,2,128,128]{3,2,1,0:T(8,128)S(1)}, f32[12,2,128,128]{3,2,1,0:T(8,128)}, u32[]{:S(2)}) copy-start(f32[12,2,128,128]{3,2,1,0:T(8,128)} %param.19) | copy-start | bytes 4718596
  7.2 191.4 %reduce-scatter.2.cloned.1.call-start = ((), (), s32[]{:S(2)}) async-start(), calls=%async_computation.1 | async-start | bytes 4718592 | tf_op jit(solution)/shard_map/reduce_scatter | solution.py:252
  7.2 82.5 %collective-permute-start = (f32[12,2,128,128]{3,2,1,0:T(8,128)}, f32[12,2,128,128]{3,2,1,0:T(8,128)}, u32[]{:S(2)}, u32[]{:S(2)}) collective-permute-start(f32[12,2,128,128]{3,2,1,0:T(8,128)} %param.19), channel_id=1, source_target_pairs={{0,16},{8,24},{16,32},{24,40},{32,48},{40,56},{48,64},{56,72},{64,... | collective-permute-start | bytes 4718600 | tf_op jit(solution)/shard_map/ppermute | solution.py:212
  14.0 109.5 %collective-permute-start.1 = (f32[12,2,128,128]{3,2,1,0:T(8,128)}, f32[12,2,128,128]{3,2,1,0:T(8,128)}, u32[]{:S(2)}, u32[]{:S(2)}) collective-permute-start(f32[12,2,128,128]{3,2,1,0:T(8,128)} %param.19), channel_id=1, source_target_pairs={{0,8},{8,16},{16,24},{24,32},{32,40},{40,48},{48,56},{56,64},{64,7... | collective-permute-start | bytes 4718600 | tf_op jit(solution)/shard_map/ppermute | solution.py:212
  18.0 109.5 %collective-permute-start.2 = (f32[12,2,128,128]{3,2,1,0:T(8,128)}, f32[12,2,128,128]{3,2,1,0:T(8,128)}, u32[]{:S(2)}, u32[]{:S(2)}) collective-permute-start(f32[12,2,128,128]{3,2,1,0:T(8,128)} %param.19), channel_id=1, source_target_pairs={{0,504},{8,0},{16,8},{24,16},{32,24},{40,32},{48,40},{56,48},{64,5... | collective-permute-start | bytes 4718600 | tf_op jit(solution)/shard_map/ppermute | solution.py:212
  25.6 104.8 %collective-permute-start.3 = (f32[12,2,128,128]{3,2,1,0:T(8,128)}, f32[12,2,128,128]{3,2,1,0:T(8,128)}, u32[]{:S(2)}, u32[]{:S(2)}) collective-permute-start(f32[12,2,128,128]{3,2,1,0:T(8,128)} %param.19), channel_id=1, source_target_pairs={{0,496},{8,504},{16,0},{24,8},{32,16},{40,24},{48,32},{56,40},{64,... | collective-permute-start | bytes 4718600 | tf_op jit(solution)/shard_map/ppermute | solution.py:212
  127.5 9.5 %copy-start.1 = (bf16[4,256,256]{2,1,0:T(8,128)(2,1)S(1)}, bf16[4,256,256]{2,1,0:T(8,128)(2,1)}, u32[]{:S(2)}) copy-start(bf16[4,256,256]{2,1,0:T(8,128)(2,1)} %v_ref.1) | copy-start | bytes 1572868
  127.5 9.6 %copy-start.2 = (bf16[4,256,256]{2,1,0:T(8,128)(2,1)S(1)}, bf16[4,256,256]{2,1,0:T(8,128)(2,1)}, u32[]{:S(2)}) copy-start(bf16[4,256,256]{2,1,0:T(8,128)(2,1)} %gate_ref.1) | copy-start | bytes 1572868
  127.5 9.6 %copy-start.3 = (bf16[4,256,128]{2,1,0:T(8,128)(2,1)S(1)}, bf16[4,256,128]{2,1,0:T(8,128)(2,1)}, u32[]{:S(2)}) copy-start(bf16[4,256,128]{2,1,0:T(8,128)(2,1)} %q_ref.1) | copy-start | bytes 786436
  127.5 9.6 %copy-start.4 = (bf16[4,256,128]{2,1,0:T(8,128)(2,1)S(1)}, bf16[4,256,128]{2,1,0:T(8,128)(2,1)}, u32[]{:S(2)}) copy-start(bf16[4,256,128]{2,1,0:T(8,128)(2,1)} %k_ref.1) | copy-start | bytes 786436
  127.5 9.6 %copy-start.5 = (f32[4,2,256]{2,1,0:T(2,128)S(1)}, f32[4,2,256]{2,1,0:T(2,128)}, u32[]{:S(2)}) copy-start(f32[4,2,256]{2,1,0:T(2,128)} %decay_ref.1) | copy-start | bytes 24580
  127.5 9.6 %copy-start.6 = (f32[4,2,256]{2,1,0:T(2,128)S(1)}, f32[4,2,256]{2,1,0:T(2,128)}, u32[]{:S(2)}) copy-start(f32[4,2,256]{2,1,0:T(2,128)} %rate_ref.1) | copy-start | bytes 24580
  127.6 9.6 %copy-start.7 = (f32[128]{0:T(128)S(1)}, f32[128]{0:T(128)}, u32[]{:S(2)}) copy-start(f32[128]{0:T(128)} %param.20) | copy-start | bytes 1540
  156.3 3.2 %copy-start.9 = (s32[4]{0:T(128)S(1)}, s32[4]{0:T(128)}, u32[]{:S(2)}) copy-start(s32[4]{0:T(128)} %param.25) | copy-start | bytes 52
  161.1 16.5 %collective-permute-start.7 = (bf16[4,2,128,128]{3,2,1,0:T(8,128)(2,1)S(1)}, bf16[4,2,128,128]{3,2,1,0:T(8,128)(2,1)S(1)}, u32[]{:S(2)}, u32[]{:S(2)}) collective-permute-start(bf16[4,2,128,128]{3,2,1,0:T(8,128)(2,1)S(1)} %get-tuple-element.10), channel_id=1, source_target_pairs={{0,16},{8,24},{16,32},{24,40},{32,48},{40,56},{48,64},{56,72},{64,... | collective-permute-start | bytes 786440 | tf_op jit(solution)/shard_map/ppermute | solution.py:212
  163.0 19.0 %collective-permute-start.6 = (bf16[4,2,128,128]{3,2,1,0:T(8,128)(2,1)S(1)}, bf16[4,2,128,128]{3,2,1,0:T(8,128)(2,1)S(1)}, u32[]{:S(2)}, u32[]{:S(2)}) collective-permute-start(bf16[4,2,128,128]{3,2,1,0:T(8,128)(2,1)S(1)} %get-tuple-element.9), channel_id=1, source_target_pairs={{0,8},{8,16},{16,24},{24,32},{32,40},{40,48},{48,56},{56,64},{64,7... | collective-permute-start | bytes 786440 | tf_op jit(solution)/shard_map/ppermute | solution.py:212
  164.9 17.0 %collective-permute-start.5 = (bf16[4,2,128,128]{3,2,1,0:T(8,128)(2,1)S(1)}, bf16[4,2,128,128]{3,2,1,0:T(8,128)(2,1)S(1)}, u32[]{:S(2)}, u32[]{:S(2)}) collective-permute-start(bf16[4,2,128,128]{3,2,1,0:T(8,128)(2,1)S(1)} %get-tuple-element.7), channel_id=1, source_target_pairs={{0,504},{8,0},{16,8},{24,16},{32,24},{40,32},{48,40},{56,48},{64,5... | collective-permute-start | bytes 786440 | tf_op jit(solution)/shard_map/ppermute | solution.py:212
  171.6 15.6 %collective-permute-start.4 = (bf16[4,2,128,128]{3,2,1,0:T(8,128)(2,1)S(1)}, bf16[4,2,128,128]{3,2,1,0:T(8,128)(2,1)S(1)}, u32[]{:S(2)}, u32[]{:S(2)}) collective-permute-start(bf16[4,2,128,128]{3,2,1,0:T(8,128)(2,1)S(1)} %get-tuple-element.6), channel_id=1, source_target_pairs={{0,496},{8,504},{16,0},{24,8},{32,16},{40,24},{48,32},{56,40},{64,... | collective-permute-start | bytes 786440 | tf_op jit(solution)/shard_map/ppermute | solution.py:212
Sparse Core Ops, SparseCore 0:
  159.7 38.8 reduce-scatter.1

commit v2 on v1

--- a/solution.py
+++ b/solution.py
@@ -1,3 +1,5 @@
+import functools
+
 import jax
 import jax.numpy as jnp
 from jax import lax
@@ -9,6 +11,10 @@
 DV = 128
 REACH = 2
 SMALL = 8
+MESH = pl.DeviceIdType.MESH
+OFFSETS = (-2, 2, -1, 1)
+CORE, PAIR, CROSS, FAR = range(4)
+
 
 def split(x):
     hi = x.astype(jnp.bfloat16)
@@ -170,46 +176,304 @@
     return (attended * scale * gain_gate_ref[slot]).astype(jnp.bfloat16), end
 
 
-def delta_kernel(q_ref, k_ref, v_ref, gate_ref, decay_ref, rate_ref, gain_ref, start_ref, normed_ref, end_ref, zhi_ref, zlo_ref, base_ref, gain_gate_ref):
+def layer_kernel(
+    workers,
+    owner_ref,
+    node_ref,
+    prefix_ref,
+    slot_ref,
+    gain_ref,
+    q_hbm,
+    k_hbm,
+    v_hbm,
+    gate_hbm,
+    decay_hbm,
+    rate_hbm,
+    cache_hbm,
+    proj_hbm,
+    mixed_ref,
+    end_ref,
+    q_ref,
+    k_ref,
+    v_ref,
+    gate_ref,
+    decay_ref,
+    rate_ref,
+    cache_ref,
+    zhi_ref,
+    zlo_ref,
+    base_ref,
+    gain_gate_ref,
+    info_ref,
+    told_ref,
+    told_smem,
+    lent_ref,
+    borrowed_ref,
+    own_end_ref,
+    sent_end_ref,
+    got_end_ref,
+    weight_ref,
+    normed_ref,
+    kept_ref,
+    passed_ref,
+    got_ref,
+    load_sem,
+    weight_load_sem,
+    told_sem,
+    info_send,
+    info_recv,
+    lend_send,
+    lend_recv,
+    end_send,
+    end_recv,
+    weight_send,
+    weight_recv,
+    normed_send,
+    normed_recv,
+    partial_send,
+    partial_recv,
+):
+    requests, tokens = q_ref.shape[:2]
     heads = decay_ref.shape[1]
-
-    @pl.loop(0, q_ref.shape[0])
-    def _(r):
-        prepare(r, q_ref, k_ref, v_ref, gate_ref, decay_ref, rate_ref, gain_ref, zhi_ref, zlo_ref, base_ref, gain_gate_ref)
-
-    @pl.loop(0, q_ref.shape[0])
-    def _(r):
+    width = heads * DV
+    slots = cache_ref.shape[0]
+    worker = lax.axis_index("worker")
+    tensor = lax.axis_index("tensor")
+    chip, core = tensor // 2, tensor % 2
+    pair_chip = chip + 1 - 2 * (chip % 2)
+    far_chip = 3 - chip
+    near = [(lax.rem(worker + workers + o, workers), tensor) for o in OFFSETS]
+    side = [
+        (worker, 2 * chip + 1 - core),
+        (worker, 2 * pair_chip + core),
+        (worker, 2 * pair_chip + 1 - core),
+        (worker, 2 * far_chip + core),
+    ]
+
+    def remote(src, dst, send, recv, device):
+        return pltpu.make_async_remote_copy(
+            src_ref=src, dst_ref=dst, send_sem=send, recv_sem=recv, device_id=device, device_id_type=MESH
+        )
+
+    loads = [
+        pltpu.make_async_copy(src, dst, load_sem.at[i])
+        for i, (src, dst) in enumerate(
+            (
+                (q_hbm, q_ref),
+                (k_hbm, k_ref),
+                (v_hbm, v_ref),
+                (decay_hbm, decay_ref),
+                (rate_hbm, rate_ref),
+                (gate_hbm, gate_ref),
+                (cache_hbm, cache_ref),
+            )
+        )
+    ]
+    for load in loads:
+        load.start()
+
+    def columns(index):
+        return pl.ds(pl.multiple_of(index * width, width), width)
+
+    def far_of(index):
+        return 2 * (3 - index // 2) + index % 2
+
+    weight_loads = [
+        pltpu.make_async_copy(
+            proj_hbm.at[:, columns(index)], weight_ref.at[0, :, pl.ds(part * width, width)], weight_load_sem.at[part]
+        )
+        for part, index in enumerate((tensor, far_of(tensor)))
+    ]
+    for load in weight_loads:
+        load.start()
+
+    lane = iota((8, 128), 1)
+    block = jnp.zeros((8, 128), jnp.int32)
+    for part, ref in enumerate((owner_ref, node_ref, prefix_ref, slot_ref)):
+        for i in range(requests):
+            block = jnp.where(lane == part * requests + i, ref[i], block)
+    info_ref[...] = block
+
+    barrier = pltpu.get_barrier_semaphore()
+    for device in near + side:
+        pl.semaphore_signal(barrier, inc=1, device_id=device, device_id_type=MESH)
+    pl.semaphore_wait(barrier, len(near) + len(side))
+
+    def opposite(n):
+        return n ^ 1
+
+    infos = [
+        remote(info_ref, told_ref.at[opposite(n)], info_send.at[n], info_recv.at[opposite(n)], near[n])
+        for n in range(4)
+    ]
+    for copy in infos:
+        copy.start()
+
+    weights = []
+    for kind in (CORE, PAIR, CROSS):
+        index = side[kind][1]
+        for part, target in enumerate((index, far_of(index))):
+            n = 2 * kind + part
+            weights.append(
+                remote(
+                    proj_hbm.at[:, columns(target)],
+                    weight_ref.at[kind + 1, :, pl.ds(part * width, width)],
+                    weight_send.at[n],
+                    weight_recv.at[n],
+                    side[kind],
+                )
+            )
+    for copy in weights:
+        copy.start()
+
+    def lend(n, i):
+        return remote(
+            lent_ref.at[n, i], borrowed_ref.at[opposite(n), i], lend_send.at[n, i], lend_recv.at[opposite(n), i], near[n]
+        )
+
+    def borrow(n, i):
+        return remote(
+            lent_ref.at[n, i], borrowed_ref.at[n, i], lend_send.at[n, i], lend_recv.at[n, i], near[n]
+        )
+
+    def send_end(n, i):
+        return remote(
+            sent_end_ref.at[i], got_end_ref.at[opposite(n), i], end_send.at[n, i], end_recv.at[opposite(n), i], near[n]
+        )
+
+    def get_end(n, i):
+        return remote(sent_end_ref.at[i], got_end_ref.at[n, i], end_send.at[n, i], end_recv.at[n, i], near[n])
+
+    def send_normed(kind, i):
+        source = 2 if kind == CROSS else 0
+        device = side[PAIR] if kind == PAIR else side[CORE]
+        return remote(
+            normed_ref.at[i, source],
+            normed_ref.at[i, kind + 1],
+            normed_send.at[kind, i],
+            normed_recv.at[kind, i],
+            device,
+        )
+
+    def send_partial(i):
+        return remote(passed_ref.at[i], got_ref.at[i], partial_send.at[i], partial_recv.at[i], side[FAR])
+
+    def answer():
+        for n in range(4):
+            remote(info_ref, told_ref.at[n], info_send.at[n], info_recv.at[n], near[n]).wait_recv()
+        fetch = pltpu.make_async_copy(told_ref, told_smem, told_sem)
+        fetch.start()
+        fetch.wait()
+        loads[6].wait()
+        for i in range(requests):
+            for n in range(4):
+                node = jnp.clip(told_smem[n, 0, requests + i], 0, slots - 1)
+                lent_ref[n, i] = cache_ref[node].astype(jnp.bfloat16)
+                lend(n, i).start()
+
+    def complete(i):
+        for n in range(4):
+            borrow(n, i).wait_recv()
+        move = lax.rem(owner_ref[i] - worker + workers + REACH, workers) - REACH
+        node = jnp.clip(node_ref[i], 0, slots - 1)
+        cached = prefix_ref[i] > 0
         for h in range(heads):
-            normed, end = finish(
-                r * heads + h, start_ref[r, h].astype(jnp.bfloat16), zhi_ref, zlo_ref, base_ref, gain_gate_ref
+            start = cache_ref[node, h].astype(jnp.bfloat16)
+            for n, offset in enumerate(OFFSETS):
+                start = jnp.where(move == offset, borrowed_ref[n, i, h], start)
+            start = jnp.where(cached, start, jnp.zeros_like(start))
+            normed, end = finish(i * heads + h, start, zhi_ref, zlo_ref, base_ref, gain_gate_ref)
+            normed_ref[i, 0, :, h * DV : (h + 1) * DV] = normed
+            own_end_ref[i, h] = end
+            sent_end_ref[i, h] = end.astype(jnp.bfloat16)
+        send_normed(PAIR, i).start()
+        send_normed(CORE, i).start()
+        for n in range(4):
+            send_end(n, i).start()
+
+    def forward(i):
+        send_normed(PAIR, i).wait_recv()
+        send_normed(CROSS, i).start()
+
+    def project(i):
+        send_normed(CORE, i).wait_recv()
+        send_normed(CROSS, i).wait_recv()
+        total = dot1(normed_ref[i, 0], weight_ref[0])
+        for source in range(1, 4):
+            total = total + dot1(normed_ref[i, source], weight_ref[source])
+        kept_ref[i] = total[:, :width]
+        passed_ref[i] = total[:, width:].astype(jnp.bfloat16)
+        send_partial(i).start()
+
+    def add(i):
+        send_partial(i).wait_recv()
+        mixed_ref[i] = (kept_ref[i] + got_ref[i].astype(jnp.float32)).astype(jnp.bfloat16)
+
+    for load in loads[:6]:
+        load.wait()
+
+    @pl.loop(0, requests + 4)
+    def _(step):
+        @pl.when(step < requests)
+        def _():
+            prepare(
+                step, q_ref, k_ref, v_ref, gate_ref, decay_ref, rate_ref, gain_ref, zhi_ref, zlo_ref, base_ref, gain_gate_ref
             )
-            normed_ref[r, :, h * DV : (h + 1) * DV] = normed
-            end_ref[r, h] = end
-
-
-def delta(q, k, v, gate, decay, rate, gain, start):
-    requests, tokens = q.shape[:2]
-    heads = decay.shape[1]
-    return pl.pallas_call(
-        delta_kernel,
-        out_shape=(
-            jax.ShapeDtypeStruct(v.shape, jnp.bfloat16),
-            jax.ShapeDtypeStruct(start.shape, jnp.float32),
-        ),
-        scratch_shapes=[
-            pltpu.VMEM((requests * heads, tokens + DK, DK), jnp.bfloat16),
-            pltpu.VMEM((requests * heads, tokens + DK, DK), jnp.bfloat16),
-            pltpu.VMEM((requests * heads, tokens + DK, DV), jnp.float32),
-            pltpu.VMEM((requests * heads, tokens, DV), jnp.float32),
-        ],
-        compiler_params=pltpu.CompilerParams(vmem_limit_bytes=48 * 1024 * 1024),
-        name="delta",
-    )(q, k, v, gate, decay, rate, gain, start)
-
-
-def shifted(x, axis, by):
-    devices = lax.axis_size(axis)
-    return lax.ppermute(x, axis, [(i, (i + by) % devices) for i in range(devices)])
+
+        @pl.when(step == 0)
+        def _():
+            answer()
+
+        @pl.when((step >= 1) & (step < requests + 1))
+        def _():
+            complete(step - 1)
+
+        @pl.when((step >= 2) & (step < requests + 2))
+        def _():
+            forward(step - 2)
+
+        @pl.when(step == 3)
+        def _():
+            for load in weight_loads:
+                load.wait()
+            for copy in weights:
+                copy.wait_recv()
+
+        @pl.when((step >= 3) & (step < requests + 3))
+        def _():
+            project(step - 3)
+
+        @pl.when(step >= 4)
+        def _():
+            add(step - 4)
+
+    for i in range(requests):
+        for n in range(4):
+            get_end(n, i).wait_recv()
+    for target in range(requests):
+        row = worker * requests + target
+        mine, theirs = jnp.int32(0), jnp.int32(0)
+        kept = jnp.bool_(False)
+        for i in range(requests):
+            here = slot_ref[i] == row
+            kept = kept | here
+            mine = jnp.where(here, i, mine)
+            for n in range(4):
+                theirs = jnp.where(told_smem[n, 0, 3 * requests + i] == row, n * requests + i, theirs)
+        for h in range(heads):
+            end_ref[target, h] = jnp.where(
+                kept, own_end_ref[mine, h], got_end_ref[theirs // requests, theirs % requests, h].astype(jnp.float32)
+            )
+
+    for copy in infos + weights:
+        copy.wait_send()
+    for i in range(requests):
+        for n in range(4):
+            lend(n, i).wait_send()
+            send_end(n, i).wait_send()
+        for kind in (CORE, PAIR, CROSS):
+            send_normed(kind, i).wait_send()
+        send_partial(i).wait_send()
 
 
 def on_device(
@@ -227,45 +491,83 @@
     prefix_len,
     write_slot,
 ):
-    requests_here, length = queries.shape[:2]
-    head_count = log_decay.shape[1]
-    slot_count = cache_states.shape[0]
-    workers = lax.axis_size("worker")
-    worker_id = lax.axis_index("worker")
-    cached = prefix_len > 0
-    relative = (hit_owner - worker_id + workers + REACH) % workers - REACH
-    pieces = []
-    for offset in range(-REACH, REACH + 1):
-        if offset == 0:
-            pieces.append(cache_states)
-        else:
-            pieces.append(shifted(cache_states, "worker", -offset))
-    window = jnp.concatenate(pieces, axis=0)
-    start_state = jnp.take(window, (relative + REACH) * slot_count + hit_node, axis=0)
-    start_state = jnp.where(cached[:, None, None, None], start_state, 0.0)
-    normed, running_state = delta(
-        queries, key_heads, values_in, out_gate, log_decay, write_rate, norm_gain[None], start_state
+    requests, tokens = queries.shape[:2]
+    heads = log_decay.shape[1]
+    width = heads * DV
+    state = cache_states.shape[1:]
+    smem = pl.BlockSpec(memory_space=pltpu.SMEM)
+    vmem = pl.BlockSpec(memory_space=pltpu.VMEM)
+    anywhere = pl.BlockSpec(memory_space=pltpu.HBM)
+    low, wide = jnp.bfloat16, jnp.float32
+    dma = pltpu.SemaphoreType.DMA
+    return pl.pallas_call(
+        functools.partial(layer_kernel, lax.axis_size("worker")),
+        out_shape=(
+            jax.ShapeDtypeStruct((requests, tokens, width), low),
+            jax.ShapeDtypeStruct((requests, *state), wide),
+        ),
+        in_specs=[smem] * 4 + [vmem] + [anywhere] * 8,
+        out_specs=(vmem, vmem),
+        scratch_shapes=[
+            pltpu.VMEM(queries.shape, low),
+            pltpu.VMEM(key_heads.shape, low),
+            pltpu.VMEM(values_in.shape, low),
+            pltpu.VMEM(out_gate.shape, low),
+            pltpu.VMEM(log_decay.shape, wide),
+            pltpu.VMEM(write_rate.shape, wide),
+            pltpu.VMEM(cache_states.shape, wide),
+            pltpu.VMEM((requests * heads, tokens + DK, DK), low),
+            pltpu.VMEM((requests * heads, tokens + DK, DK), low),
+            pltpu.VMEM((requests * heads, tokens + DK, DV), wide),
+            pltpu.VMEM((requests * heads, tokens, DV), wide),
+            pltpu.VMEM((8, 128), jnp.int32),
+            pltpu.VMEM((4, 8, 128), jnp.int32),
+            pltpu.SMEM((4, 8, 128), jnp.int32),
+            pltpu.VMEM((4, requests, *state), low),
+            pltpu.VMEM((4, requests, *state), low),
+            pltpu.VMEM((requests, *state), wide),
+            pltpu.VMEM((requests, *state), low),
+            pltpu.VMEM((4, requests, *state), low),
+            pltpu.VMEM((4, width, 2 * width), low),
+            pltpu.VMEM((requests, 4, tokens, width), low),
+            pltpu.VMEM((requests, tokens, width), wide),
+            pltpu.VMEM((requests, tokens, width), low),
+            pltpu.VMEM((requests, tokens, width), low),
+            dma((7,)),
+            dma((2,)),
+            dma,
+            dma((4,)),
+            dma((4,)),
+            dma((4, requests)),
+            dma((4, requests)),
+            dma((4, requests)),
+            dma((4, requests)),
+            dma((6,)),
+            dma((6,)),
+            dma((3, requests)),
+            dma((3, requests)),
+            dma((requests,)),
+            dma((requests,)),
+        ],
+        compiler_params=pltpu.CompilerParams(
+            collective_id=0, has_side_effects=True, vmem_limit_bytes=60 * 1024 * 1024
+        ),
+        name="layer",
+    )(
+        hit_owner,
+        hit_node,
+        prefix_len,
+        write_slot,
+        norm_gain[None],
+        queries,
+        key_heads,
+        values_in,
+        out_gate,
+        log_decay,
+        write_rate,
+        cache_states,
+        out_proj,
     )
-    partial_value = jnp.dot(
-        normed.reshape(requests_here * length, head_count * DV), out_proj, preferred_element_type=jnp.float32
-    ).reshape(requests_here, length, out_proj.shape[1])
-    mixed = lax.psum_scatter(
-        partial_value.astype(jnp.bfloat16), "tensor", scatter_dimension=2, tiled=True
-    )
-    target_worker = write_slot // requests_here
-    target_lane = write_slot % requests_here
-    target_move = (target_worker - worker_id + workers + REACH) % workers - REACH
-    lane_ids = jnp.arange(requests_here, dtype=jnp.int32)
-    end_states = jnp.zeros_like(running_state)
-    for offset in range(-REACH, REACH + 1):
-        routed = (target_move == offset)[:, None] & (target_lane[:, None] == lane_ids[None, :])
-        packed = jnp.sum(
-            jnp.where(routed[:, :, None, None, None], running_state[:, None], 0.0), axis=0
-        )
-        if offset != 0:
-            packed = shifted(packed.astype(jnp.bfloat16), "worker", offset).astype(packed.dtype)
-        end_states = end_states + packed
-    return (mixed, end_states)
 
 
 def solution(mesh):

time: 207 us -> 66.9 us (0.32)
  waiting for transfers between devices: 111 us -> 0 us
  Pallas kernels: 19.2 us -> 61.9 us
  starting transfers between devices: 37.5 us -> 0 us
  between operations: 14.3 us -> 0.64 us
  local copies, waits for them, and re-layouts: 16.1 us -> 3.74 us
  other arithmetic: 3.88 us -> 0 us
  matrix products: 3.21 us -> 0 us
    ppermute x8 -> x0, waiting for transfers between devices: 101 us -> none  [shifted(): lax.ppermute(x, axis, [(i, (i + by) % devices) for i in range(devices)])]
    pallas_call x1, Pallas kernels: 19.2 us -> 61.9 us  [on_device(): pl.pallas_call(functools.partial(layer_kernel, lax.axis_size('worker')),...]
    ppermute x8 -> x0, starting transfers between devices: 37.4 us -> none  [shifted(): lax.ppermute(x, axis, [(i, (i + by) % devices) for i in range(devices)])]
    reduce_scatter x1 -> x0, waiting for transfers between devices: 10.5 us -> none  [on_device(): lax.psum_scatter(partial_value.astype(jnp.bfloat16), 'tensor', scatter_di...]
    unnamed x24 -> x2, local copies, waits for them, and re-layouts: 9.56 us -> 3.74 us
    gather x1 -> x0, local copies, waits for them, and re-layouts: 3.81 us -> none  [on_device(): jnp.take(window, (relative + REACH) * slot_count + hit_node, axis=0)]
    dot_general x1 -> x0, matrix products: 3.21 us -> none  [on_device(): jnp.dot(normed.reshape(requests_here * length, head_count * DV), out_proj...]
    concatenate x1 -> x0, local copies, waits for them, and re-layouts: 2.71 us -> none  [on_device(): window = jnp.concatenate(pieces, axis=0)]
  transfers between devices with their start and end apart: 9 -> 0, of which waited for: 6 -> 0; matrix products, arithmetic and copies ran while one was open for 6% -> 0% of each run, Pallas kernels for 0% -> 0%
where the time goes in v2:
time: 66.9 us; the launch traced here: 66.3 us
  Pallas kernels  61.9 us (93%)
  local copies, waits for them, and re-layouts  3.74 us (6%)
    pallas_call x1, Pallas kernels, on_device(): pl.pallas_call(functools.partial(layer_kernel, lax.axis_size('worker')),...  61.9 us
    unnamed x2, local copies, waits for them, and re-layouts  3.74 us

profile of v2, /device:TPU:1, one launch (start us, length us, event | category | flops | bytes accessed | tf_op | source)
XLA Modules:
  0.0 66.3 jit_solution(11455653498825367491)
XLA Ops:
  0.6 61.9 %layer.1 = (bf16[4,256,256]{2,1,0:T(8,128)(2,1)}, f32[4,2,128,128]{3,2,1,0:T(8,128)}) custom-call(s32[4]{0:T(128)} %owner_ref.1, s32[4]{0:T(128)} %node_ref.1, s32[4]{0:T(128)} %prefix_ref.1, s32[4]{0:T(128)} %slot_ref.1, f32[1,128]{1,0:T(1,128)} %bitcast.1, bf16[4,256,128]{2,1,0:T(8,128)(2,1)} %q_hbm.1, bf16[4,256,128]{2,1,0:T(8,128)(2,1)} %k_hbm.1, ...), custom_call_target="tpu_custom_call" | custom-call | tf_op jit(solution)/shard_map/layer/pallas_call | solution.py:503
  62.5 1.9 %copy.17 = bf16[4,256,256]{2,1,0:T(8,128)(2,1)} copy(bf16[4,256,256]{2,1,0:T(8,128)(2,1)} %get-tuple-element.4) | data formatting | bytes 1048576
  64.4 1.9 %copy.18 = f32[4,2,128,128]{3,2,1,0:T(8,128)} copy(f32[4,2,128,128]{3,2,1,0:T(8,128)} %get-tuple-element.5) | data formatting | bytes 1048576

commit v3 on v2

v3 whole, which is shorter than its diff:
```python
import functools

import jax
import jax.numpy as jnp
from jax import lax
from jax.experimental import pallas as pl
from jax.experimental.pallas import tpu as pltpu
from jax.sharding import PartitionSpec as P

DK = 128
DV = 128
REACH = 2
SMALL = 8
MESH = pl.DeviceIdType.MESH
OFFSETS = (-2, 2, -1, 1)
TWIN, MATE, CROSS = range(3)


def split(x):
    hi = x.astype(jnp.bfloat16)
    return hi, (x - hi.astype(jnp.float32)).astype(jnp.bfloat16)


def dot1(a, b):
    return jnp.dot(a, b, preferred_element_type=jnp.float32)


def dot3(a, b):
    (a_hi, a_lo), (b_hi, b_lo) = a, b
    return dot1(jnp.concatenate([a_hi, a_lo, a_hi], axis=1), jnp.concatenate([b_hi, b_hi, b_lo], axis=0))


def dot_nt(a, b):
    return lax.dot_general(a, b, (((1,), (1,)), ((), ())), preferred_element_type=jnp.float32)


def dot_tn(a, b):
    return lax.dot_general(a, b, (((0,), (0,)), ((), ())), preferred_element_type=jnp.float32)


def iota(shape, dim):
    return lax.broadcasted_iota(jnp.int32, shape, dim)


def solve_small(compact):
    rows, lanes = compact.shape
    place = iota((rows, lanes), 1) % SMALL
    inverse = jnp.where(place == iota((rows, lanes), 0) % SMALL, 1.0, 0.0)
    for j in range(SMALL - 1):
        column = jnp.where(place == j, compact, 0.0)
        if j:
            column = pltpu.roll(column, lanes - j, 1)
        for step in (1, 2, 4):
            column = column + pltpu.roll(column, step, 1)
        groups = inverse.reshape(rows // SMALL, SMALL, lanes)
        row = jnp.broadcast_to(groups[:, j : j + 1, :], groups.shape).reshape(rows, lanes)
        inverse = inverse - column * row
    return inverse


def invert_unit_lower(systems):
    n = systems[0].shape[0]
    own = iota((n, n), 1) // SMALL == iota((n, n), 0) // SMALL
    compact = [
        jnp.sum(jnp.where(own, system, 0.0).reshape(n // SMALL, SMALL, n), axis=0) for system in systems
    ]
    small = solve_small(jnp.concatenate(compact, axis=0))
    inverses = []
    for i in range(len(systems)):
        block = small[i * SMALL : (i + 1) * SMALL]
        wide = jnp.broadcast_to(block[None], (n // SMALL, SMALL, n)).reshape(n, n)
        inverses.append(jnp.where(own, wide, 0.0))
    parts = [split(system) for system in systems]
    size = SMALL
    while size < n:
        row, lane = iota((n, n), 0) // size, iota((n, n), 1) // size
        below = (row % 2 == 1) & (row == lane + 1)
        cut = [tuple(jnp.where(below, part, jnp.zeros_like(part)) for part in pair) for pair in parts]
        halves = [split(inverse) for inverse in inverses]
        inner = [split(dot3(x, y)) for x, y in zip(cut, halves)]
        inverses = [inverse - dot3(x, y) for inverse, x, y in zip(inverses, halves, inner)]
        size *= 2
    return inverses


def prepare(
    rs, between, q_ref, k_ref, v_ref, gate_ref, decay_ref, rate_ref, gain_ref, zhi_ref, zlo_ref, base_ref, gain_gate_ref
):
    tokens = q_ref.shape[1]
    heads = decay_ref.shape[1]
    half = tokens // 2
    row, lane = iota((half, half), 0), iota((half, half), 1)
    upto = jnp.where(iota((tokens, tokens), 0) <= iota((tokens, tokens), 1), 1.0, 0.0).astype(jnp.bfloat16)
    decay = jnp.concatenate([decay_ref[r] for r in rs], axis=0)
    hi, _ = split(decay)
    rest = decay - hi.astype(jnp.float32)
    mid, low = split(rest)
    sums = dot1(jnp.concatenate([hi, mid, low], axis=0), upto)
    count = len(rs) * heads
    runnings = sums[2 * count :] + sums[count : 2 * count] + sums[:count]
    every = [runnings] + [rate_ref[r] for r in rs]
    pad = -2 * count % 8
    if pad:
        every.append(jnp.zeros((pad, tokens), jnp.float32))
    columns = jnp.concatenate(every, axis=0).T
    chains = []
    for n, r in enumerate(rs):
        q, k = q_ref[r], k_ref[r]
        qf, kf = q.astype(jnp.float32), k.astype(jnp.float32)
        rq = lax.rsqrt(jnp.sum(qf * qf, axis=1, keepdims=True) + 1e-06) * DK ** (-0.5)
        rk = lax.rsqrt(jnp.sum(kf * kf, axis=1, keepdims=True) + 1e-06)
        first, second = dot_nt(k, k[:half]), dot_nt(k[half:], k[half:])
        scales = [
            lax.rsqrt(jnp.sum(jnp.where(row == lane, raw, 0.0), axis=0, keepdims=True) + 1e-06)
            for raw in (first[:half], second)
        ]
        kk = [
            first[:half] * (scales[0] * rk[:half]),
            first[half:] * (scales[0] * rk[half:]),
            second * (scales[1] * rk[half:]),
        ]
        first, second = dot_nt(q, k[:half]), dot_nt(q[half:], k[half:])
        qk = [
            first[:half] * (scales[0] * rq[:half]),
            first[half:] * (scales[0] * rq[half:]),
            second * (scales[1] * rq[half:]),
        ]
        for h in range(heads):
            c = n * heads + h
            chains.append((r, h, qf, kf, rq, rk, kk, qk, columns[:, c : c + 1], columns[:, count + c : count + c + 1], runnings[c : c + 1]))
    systems, crosses, reads = [], [], []
    for r, h, qf, kf, rq, rk, kk, qk, g, rate, ahead in chains:
        within = [
            jnp.exp(jnp.where(row >= lane, g[:half] - ahead[:, :half], -jnp.inf)),
            jnp.exp(g[half:] - ahead[:, :half]),
            jnp.exp(jnp.where(row >= lane, g[half:] - ahead[:, half:], -jnp.inf)),
        ]
        systems.append(jnp.where(row > lane, rate[:half] * (within[0] * kk[0]), 0.0))
        systems.append(jnp.where(row > lane, rate[half:] * (within[2] * kk[2]), 0.0))
        crosses.append(split(rate[half:] * (within[1] * kk[1])))
        reads.append([split(x * y) for x, y in zip(within, qk)])
    inverses = [split(x) for x in invert_unit_lower(systems)]
    between()
    rights = []
    for r, h, qf, kf, rq, rk, kk, qk, g, rate, ahead in chains:
        values = v_ref[r, :, h * DV : (h + 1) * DV].astype(jnp.float32)
        rights.append(jnp.concatenate([rate * values, (rate * jnp.exp(g) * rk) * kf], axis=1))
    tops = [split(dot3(x, split(y[:half]))) for x, y in zip(inverses[::2], rights)]
    rests = [y[half:] - dot3(x, top) for x, y, top in zip(crosses, rights, tops)]
    bottoms = [split(dot3(x, split(rest))) for x, rest in zip(inverses[1::2], rests)]
    solveds = [
        tuple(jnp.concatenate([x, y], axis=0) for x, y in zip(top, bottom)) for top, bottom in zip(tops, bottoms)
    ]
    read_tops = [dot3(read[0], top) for read, top in zip(reads, tops)]
    read_bottoms = [
        dot3(tuple(jnp.concatenate([x, y], axis=1) for x, y in zip(read[1], read[2])), solved)
        for read, solved in zip(reads, solveds)
    ]
    ends = []
    for (r, h, qf, kf, rq, rk, kk, qk, g, rate, ahead), solved in zip(chains, solveds):
        hi, lo = split((jnp.exp(g[tokens - 1 :] - g) * rk) * kf)
        ends.append(dot_tn(jnp.concatenate([hi, lo, hi], axis=0), jnp.concatenate([solved[0], solved[0], solved[1]], axis=0)))
    eye = iota((DK, DK), 0) == iota((DK, DK), 1)
    for (r, h, qf, kf, rq, rk, kk, qk, g, rate, ahead), top, bottom, end in zip(chains, read_tops, read_bottoms, ends):
        slot = r * heads + h
        base_ref[slot, :half] = top[:, :DV]
        base_ref[slot, half:tokens] = bottom[:, :DV]
        base_ref[slot, tokens:] = end[:, :DV]
        from_state = (jnp.exp(g) * rq) * qf - jnp.concatenate([top[:, DV:], bottom[:, DV:]], axis=0)
        to_state = jnp.where(eye, jnp.exp(g[tokens - 1 :]), 0.0) - end[:, DV:]
        z_hi, z_lo = split(jnp.concatenate([from_state, to_state], axis=0))
        zhi_ref[slot] = z_hi
        zlo_ref[slot] = z_lo
        gate = gate_ref[r, :, h * DV : (h + 1) * DV].astype(jnp.float32)
        gain_gate_ref[slot] = gain_ref[...] * (gate / (1.0 + jnp.exp(-gate)))


def finish(slots, starts, zhi_ref, zlo_ref, base_ref, gain_gate_ref):
    tokens = gain_gate_ref.shape[1]
    wholes = [
        dot1(zhi_ref[slot], start) + dot1(zlo_ref[slot], start) + base_ref[slot] for slot, start in zip(slots, starts)
    ]
    scales = [
        lax.rsqrt(jnp.mean(whole[:tokens] * whole[:tokens], axis=1, keepdims=True) + 1e-06) for whole in wholes
    ]
    normed = [
        (whole[:tokens] * scale * gain_gate_ref[slot]).astype(jnp.bfloat16)
        for slot, whole, scale in zip(slots, wholes, scales)
    ]
    return normed, [whole[tokens:] for whole in wholes]


def layer_kernel(
    workers,
    owner_ref,
    node_ref,
    prefix_ref,
    slot_ref,
    gain_ref,
    q_hbm,
    k_hbm,
    v_hbm,
    gate_hbm,
    decay_hbm,
    rate_hbm,
    cache_hbm,
    proj_hbm,
    mixed_ref,
    end_ref,
    q_ref,
    k_ref,
    v_ref,
    gate_ref,
    decay_ref,
    rate_ref,
    cache_ref,
    zhi_ref,
    zlo_ref,
    base_ref,
    gain_gate_ref,
    info_ref,
    told_ref,
    told_smem,
    hop_out_ref,
    hop_in_ref,
    lent_ref,
    borrowed_ref,
    sent_end_ref,
    got_end_ref,
    weight_ref,
    normed_ref,
    kept_ref,
    passed_ref,
    got_ref,
    load_sem,
    weight_load_sem,
    told_sem,
    info_send,
    info_recv,
    hop_send,
    hop_recv,
    lend_send,
    lend_recv,
    end_send,
    end_recv,
    weight_send,
    weight_recv,
    normed_send,
    normed_recv,
    partial_send,
    partial_recv,
):
    requests, tokens = q_ref.shape[:2]
    heads = decay_ref.shape[1]
    width = heads * DV
    slots = cache_ref.shape[0]
    worker = lax.axis_index("worker")
    tensor = lax.axis_index("tensor")
    chip, core = tensor // 2, tensor % 2

    def paired(index, way):
        there = index // 2
        mate = 3 - there if way else there + 1 - 2 * (there % 2)
        return 2 * mate + index % 2

    near = [(lax.rem(worker + workers + o, workers), tensor) for o in OFFSETS]
    twin = 2 * chip + 1 - core
    sides = [(twin, paired(tensor, way), paired(twin, way)) for way in range(2)]
    others = [twin, *sides[0][1:], *sides[1][1:]]

    def remote(src, dst, send, recv, device):
        return pltpu.make_async_remote_copy(
            src_ref=src, dst_ref=dst, send_sem=send, recv_sem=recv, device_id=device, device_id_type=MESH
        )

    loads = [
        pltpu.make_async_copy(src, dst, load_sem.at[i])
        for i, (src, dst) in enumerate(
            (
                (q_hbm, q_ref),
                (k_hbm, k_ref),
                (v_hbm, v_ref),
                (decay_hbm, decay_ref),
                (rate_hbm, rate_ref),
                (gate_hbm, gate_ref),
                (cache_hbm, cache_ref),
            )
        )
    ]
    for load in loads:
        load.start()

    def columns(index):
        return pl.ds(pl.multiple_of(index * width, width), width)

    weight_loads = [
        pltpu.make_async_copy(
            proj_hbm.at[:, columns(index)],
            weight_ref.at[way, 0, :, pl.ds(part * width, width)],
            weight_load_sem.at[way, part],
        )
        for way in range(2)
        for part, index in enumerate((tensor, paired(tensor, 1 - way)))
    ]
    for load in weight_loads:
        load.start()

    lane = iota((8, 128), 1)
    block = jnp.zeros((8, 128), jnp.int32)
    for part, ref in enumerate((owner_ref, node_ref, prefix_ref, slot_ref)):
        for i in range(requests):
            block = jnp.where(lane == part * requests + i, ref[i], block)
    info_ref[...] = block

    barrier = pltpu.get_barrier_semaphore()
    for device in near + [(worker, index) for index in others]:
        pl.semaphore_signal(barrier, inc=1, device_id=device, device_id_type=MESH)
    pl.semaphore_wait(barrier, len(near) + len(others))

    def opposite(n):
        return n ^ 1

    infos = [
        remote(info_ref, told_ref.at[opposite(n)], info_send.at[n], info_recv.at[opposite(n)], near[n])
        for n in range(4)
    ]
    for copy in infos:
        copy.start()

    weights = []
    for kind in (MATE, CROSS, TWIN):
        for part in range(2):
            for way in range(2):
                index = sides[way][kind]
                target = paired(index, 1 - way) if part else index
                weights.append(
                    remote(
                        proj_hbm.at[:, columns(target)],
                        weight_ref.at[way, kind + 1, :, pl.ds(part * width, width)],
                        weight_send.at[way, kind, part],
                        weight_recv.at[way, kind, part],
                        (worker, index),
                    )
                )
    for copy in weights:
        copy.start()

    def hop(way, i):
        return remote(
            hop_out_ref.at[way, i], hop_in_ref.at[way, i], hop_send.at[way, i], hop_recv.at[way, i], near[2 + way]
        )

    def lend(way, i):
        return remote(
            lent_ref.at[way, i], borrowed_ref.at[way, i], lend_send.at[way, i], lend_recv.at[way, i], near[2 + way]
        )

    def send_end(way, i):
        return remote(
            sent_end_ref.at[i], got_end_ref.at[2 + way, i], end_send.at[2 + way, i], end_recv.at[2 + way, i], near[2 + way]
        )

    def pass_end(way, i):
        return remote(
            got_end_ref.at[2 + way, i], got_end_ref.at[way, i], end_send.at[way, i], end_recv.at[way, i], near[2 + way]
        )

    def send_normed(kind, i):
        source = 2 if kind == CROSS else 0
        index = sides[i % 2][MATE] if kind == MATE else twin
        return remote(
            normed_ref.at[i, source],
            normed_ref.at[i, kind + 1],
            normed_send.at[kind, i],
            normed_recv.at[kind, i],
            (worker, index),
        )

    def send_partial(i):
        index = sides[1 - i % 2][MATE]
        return remote(passed_ref.at[i], got_ref.at[i], partial_send.at[i], partial_recv.at[i], (worker, index))

    def wanted(n, i):
        return cache_ref[jnp.clip(told_smem[n, 0, requests + i], 0, slots - 1)].astype(jnp.bfloat16)

    def answer():
        for n in range(4):
            remote(info_ref, told_ref.at[n], info_send.at[n], info_recv.at[n], near[n]).wait_recv()
        fetch = pltpu.make_async_copy(told_ref, told_smem, told_sem)
        fetch.start()
        fetch.wait()
        loads[6].wait()
        for i in range(requests):
            for way in range(2):
                hop_out_ref[way, i] = wanted(way, i)
                hop(way, i).start()

    def merge(i):
        for way in range(2):
            hop(way, i).wait_recv()
            mine = told_smem[2 + way, 0, i] == worker
            lent_ref[way, i] = jnp.where(mine, wanted(2 + way, i), hop_in_ref[way, i])
            lend(way, i).start()

    def complete(i):
        for way in range(2):
            lend(way, i).wait_recv()
        move = lax.rem(owner_ref[i] - worker + workers + REACH, workers) - REACH
        node = jnp.clip(node_ref[i], 0, slots - 1)
        cached = prefix_ref[i] > 0
        starts = []
        for h in range(heads):
            start = cache_ref[node, h].astype(jnp.bfloat16)
            start = jnp.where(move < 0, borrowed_ref[1, i, h], start)
            start = jnp.where(move > 0, borrowed_ref[0, i, h], start)
            starts.append(jnp.where(cached, start, jnp.zeros_like(start)))
        slots_here = [i * heads + h for h in range(heads)]
        normed, ends = finish(slots_here, starts, zhi_ref, zlo_ref, base_ref, gain_gate_ref)
        for h in range(heads):
            normed_ref[i, 0, :, h * DV : (h + 1) * DV] = normed[h]
            sent_end_ref[i, h] = ends[h].astype(jnp.bfloat16)
        send_normed(MATE, i).start()
        send_normed(TWIN, i).start()
        for way in range(2):
            send_end(way, i).start()

    def relay(i):
        for way in range(2):
            send_end(way, i).wait_recv()
            pass_end(way, i).start()

    def forward(i):
        send_normed(MATE, i).wait_recv()
        send_normed(CROSS, i).start()

    def project(i):
        send_normed(TWIN, i).wait_recv()
        send_normed(CROSS, i).wait_recv()
        way = i % 2
        total = dot1(normed_ref[i, 0], weight_ref[way, 0])
        for source in range(1, 4):
            total = total + dot1(normed_ref[i, source], weight_ref[way, source])
        kept_ref[i] = total[:, :width]
        passed_ref[i] = total[:, width:].astype(jnp.bfloat16)
        send_partial(i).start()

    def add(i):
        send_partial(i).wait_recv()
        mixed_ref[i] = (kept_ref[i] + got_ref[i].astype(jnp.float32)).astype(jnp.bfloat16)

    for load in loads[:6]:
        load.wait()

    def ready(rs, between):
        prepare(
            rs, between, q_ref, k_ref, v_ref, gate_ref, decay_ref, rate_ref, gain_ref, zhi_ref, zlo_ref, base_ref, gain_gate_ref
        )

    def merge_first():
        merge(0)
        merge(1)

    ready([0, 1], answer)
    ready([2, 3], merge_first)
    merge(2)
    merge(3)
    complete(0)
    complete(1)
    complete(2)
    complete(3)
    for load in weight_loads:
        load.wait()
    for copy in weights:
        copy.wait_recv()
    relay(0)
    forward(0)
    relay(1)
    forward(1)
    project(0)
    relay(2)
    project(1)
    forward(2)
    relay(3)
    forward(3)
    project(2)
    project(3)
    add(0)
    add(1)
    add(2)
    for i in range(requests):
        for way in range(2):
            pass_end(way, i).wait_recv()
    for target in range(requests):
        row = worker * requests + target
        mine, theirs = jnp.int32(0), jnp.int32(0)
        kept = jnp.bool_(False)
        for i in range(requests):
            here = slot_ref[i] == row
            kept = kept | here
            mine = jnp.where(here, i, mine)
            for n in range(4):
                theirs = jnp.where(told_smem[opposite(n), 0, 3 * requests + i] == row, n * requests + i, theirs)
        end_ref[target] = jnp.where(
            kept, sent_end_ref[mine], got_end_ref[theirs // requests, theirs % requests]
        )
    add(3)

    for copy in infos + weights:
        copy.wait_send()
    for i in range(requests):
        for way in range(2):
            hop(way, i).wait_send()
            lend(way, i).wait_send()
            send_end(way, i).wait_send()
            pass_end(way, i).wait_send()
        for kind in (TWIN, MATE, CROSS):
            send_normed(kind, i).wait_send()
        send_partial(i).wait_send()


def store_kernel(mixed_ref, end_ref, mixed_hbm, end_hbm, wide_ref, mixed_sem, end_sem):
    requests = mixed_ref.shape[0]
    copies = [pltpu.make_async_copy(mixed_ref.at[i], mixed_hbm.at[i], mixed_sem.at[i]) for i in range(requests)]
    for copy in copies:
        copy.start()
    for i in range(requests):
        wide_ref[i] = end_ref[i].astype(jnp.float32)
        copies.append(pltpu.make_async_copy(wide_ref.at[i], end_hbm.at[i], end_sem.at[i]))
        copies[-1].start()
    for copy in copies:
        copy.wait()


def on_device(
    queries,
    key_heads,
    values_in,
    out_gate,
    log_decay,
    write_rate,
    cache_states,
    norm_gain,
    out_proj,
    hit_owner,
    hit_node,
    prefix_len,
    write_slot,
):
    requests, tokens = queries.shape[:2]
    heads = log_decay.shape[1]
    width = heads * DV
    state = cache_states.shape[1:]
    smem = pl.BlockSpec(memory_space=pltpu.SMEM)
    vmem = pl.BlockSpec(memory_space=pltpu.VMEM)
    anywhere = pl.BlockSpec(memory_space=pltpu.HBM)
    low, wide = jnp.bfloat16, jnp.float32
    dma = pltpu.SemaphoreType.DMA
    mixed, ends = pl.pallas_call(
        functools.partial(layer_kernel, lax.axis_size("worker")),
        out_shape=(
            pltpu.VMEM((requests, tokens, width), low),
            pltpu.VMEM((requests, *state), low),
        ),
        in_specs=[smem] * 4 + [vmem] + [anywhere] * 8,
        out_specs=(vmem, vmem),
        scratch_shapes=[
            pltpu.VMEM(queries.shape, low),
            pltpu.VMEM(key_heads.shape, low),
            pltpu.VMEM(values_in.shape, low),
            pltpu.VMEM(out_gate.shape, low),
            pltpu.VMEM(log_decay.shape, wide),
            pltpu.VMEM(write_rate.shape, wide),
            pltpu.VMEM(cache_states.shape, wide),
            pltpu.VMEM((requests * heads, tokens + DK, DK), low),
            pltpu.VMEM((requests * heads, tokens + DK, DK), low),
            pltpu.VMEM((requests * heads, tokens + DK, DV), wide),
            pltpu.VMEM((requests * heads, tokens, DV), wide),
            pltpu.VMEM((8, 128), jnp.int32),
            pltpu.VMEM((4, 8, 128), jnp.int32),
            pltpu.SMEM((4, 8, 128), jnp.int32),
            pltpu.VMEM((2, requests, *state), low),
            pltpu.VMEM((2, requests, *state), low),
            pltpu.VMEM((2, requests, *state), low),
            pltpu.VMEM((2, requests, *state), low),
            pltpu.VMEM((requests, *state), low),
            pltpu.VMEM((4, requests, *state), low),
            pltpu.VMEM((2, 4, width, 2 * width), low),
            pltpu.VMEM((requests, 4, tokens, width), low),
            pltpu.VMEM((requests, tokens, width), wide),
            pltpu.VMEM((requests, tokens, width), low),
            pltpu.VMEM((requests, tokens, width), low),
            dma((7,)),
            dma((2, 2)),
            dma,
            dma((4,)),
            dma((4,)),
            dma((2, requests)),
            dma((2, requests)),
            dma((2, requests)),
            dma((2, requests)),
            dma((4, requests)),
            dma((4, requests)),
            dma((2, 3, 2)),
            dma((2, 3, 2)),
            dma((3, requests)),
            dma((3, requests)),
            dma((requests,)),
            dma((requests,)),
        ],
        compiler_params=pltpu.CompilerParams(
            collective_id=0, has_side_effects=True, vmem_limit_bytes=48 * 1024 * 1024
        ),
        name="layer",
    )(
        *(
            pltpu.with_memory_space_constraint(x, pltpu.HBM)
            for x in (
                hit_owner,
                hit_node,
                prefix_len,
                write_slot,
                norm_gain[None],
                queries,
                key_heads,
                values_in,
                out_gate,
                log_decay,
                write_rate,
                cache_states,
                out_proj,
            )
        )
    )
    return pl.pallas_call(
        store_kernel,
        out_shape=(jax.ShapeDtypeStruct(mixed.shape, low), jax.ShapeDtypeStruct(ends.shape, wide)),
        in_specs=[vmem] * 2,
        out_specs=(anywhere, anywhere),
        scratch_shapes=[pltpu.VMEM(ends.shape, wide), dma((requests,)), dma((requests,))],
        compiler_params=pltpu.CompilerParams(vmem_limit_bytes=32 * 1024 * 1024),
        name="store",
    )(mixed, ends)


def solution(mesh):
    in_specs = (
        P("worker", None, "tensor"),
        P("worker", None, "tensor"),
        P("worker", None, "tensor"),
        P("worker", None, "tensor"),
        P("worker", "tensor", None),
        P("worker", "tensor", None),
        P("worker", "tensor", None, None),
        P(),
        P("tensor", None),
        P("worker"),
        P("worker"),
        P("worker"),
        P("worker"),
    )
    out_specs = (P("worker", None, "tensor"), P("worker", "tensor", None, None))
    return jax.shard_map(
        on_device, mesh=mesh, in_specs=in_specs, out_specs=out_specs, check_vma=False
    )
```

time: 66.9 us -> 51.8 us (0.77)
  Pallas kernels: 61.9 us -> 51 us
  local copies, waits for them, and re-layouts: 3.74 us -> 0 us
    pallas_call x1, Pallas kernels: 61.9 us -> 50 us  [on_device(): pl.pallas_call(functools.partial(layer_kernel, lax.axis_size('worker')),...]
    unnamed x2 -> x0, local copies, waits for them, and re-layouts: 3.74 us -> none
    pallas_call x0 -> x1, Pallas kernels: none -> 1.03 us  [on_device(): pl.pallas_call(store_kernel, out_shape=(jax.ShapeDtypeStruct(mixed.shape,...]
where the time goes in v3:
time: 51.8 us; the launch traced here: 51.6 us
  Pallas kernels  51 us (98%)
  between operations  0.64 us (1%)
    pallas_call x1, Pallas kernels, on_device(): pl.pallas_call(functools.partial(layer_kernel, lax.axis_size('worker')),...  50 us

profile of v3, /device:TPU:1, one launch (start us, length us, event | category | flops | bytes accessed | tf_op | source)
XLA Modules:
  0.0 51.6 jit_solution(13306608479039837710)
XLA Ops:
  0.6 50.0 %layer.1 = (bf16[4,256,256]{2,1,0:T(8,128)(2,1)S(1)}, bf16[4,2,128,128]{3,2,1,0:T(8,128)(2,1)S(1)}) custom-call(s32[4]{0:T(128)} %owner_ref.1, s32[4]{0:T(128)} %node_ref.1, s32[4]{0:T(128)} %prefix_ref.1, s32[4]{0:T(128)} %slot_ref.1, f32[1,128]{1,0:T(1,128)} %bitcast.1, bf16[4,256,128]{2,1,0:T(8,128)(2,1)} %q_hbm.1, bf16[4,256,128]{2,1,0:T(8,128)(2,1)} %k_hbm.1, ...), custom_call_target="tpu_custom_call" | custom-call | tf_op jit(solution)/shard_map/layer/pallas_call | solution.py:558
  50.6 1.0 %store.1 = (bf16[4,256,256]{2,1,0:T(8,128)(2,1)}, f32[4,2,128,128]{3,2,1,0:T(8,128)}) custom-call(bf16[4,256,256]{2,1,0:T(8,128)(2,1)S(1)} %get-tuple-element.4.mixed_ref, bf16[4,2,128,128]{3,2,1,0:T(8,128)(2,1)S(1)} %get-tuple-element.5.end_ref), custom_call_target="tpu_custom_call" | custom-call | tf_op jit(solution)/shard_map/store/pallas_call | solution.py:634

commit v4 on v3

--- a/solution.py
+++ b/solution.py
@@ -192,11 +192,11 @@
 
 def layer_kernel(
     workers,
-    owner_ref,
-    node_ref,
-    prefix_ref,
-    slot_ref,
-    gain_ref,
+    owner_hbm,
+    node_hbm,
+    prefix_hbm,
+    slot_hbm,
+    gain_hbm,
     q_hbm,
     k_hbm,
     v_hbm,
@@ -207,6 +207,11 @@
     proj_hbm,
     mixed_ref,
     end_ref,
+    owner_ref,
+    node_ref,
+    prefix_ref,
+    slot_ref,
+    gain_ref,
     q_ref,
     k_ref,
     v_ref,
@@ -232,6 +237,7 @@
     kept_ref,
     passed_ref,
     got_ref,
+    ask_sem,
     load_sem,
     weight_load_sem,
     told_sem,
@@ -251,6 +257,7 @@
     partial_recv,
 ):
     requests, tokens = q_ref.shape[:2]
+    half = tokens // 2
     heads = decay_ref.shape[1]
     width = heads * DV
     slots = cache_ref.shape[0]
@@ -273,6 +280,17 @@
             src_ref=src, dst_ref=dst, send_sem=send, recv_sem=recv, device_id=device, device_id_type=MESH
         )
 
+    barrier = pltpu.get_barrier_semaphore()
+    for device in near + [(worker, index) for index in others]:
+        pl.semaphore_signal(barrier, inc=1, device_id=device, device_id_type=MESH)
+    asks = [
+        pltpu.make_async_copy(src, dst, ask_sem.at[i])
+        for i, (src, dst) in enumerate(
+            ((owner_hbm, owner_ref), (node_hbm, node_ref), (prefix_hbm, prefix_ref), (slot_hbm, slot_ref))
+        )
+    ]
+    for ask in asks:
+        ask.start()
     loads = [
         pltpu.make_async_copy(src, dst, load_sem.at[i])
         for i, (src, dst) in enumerate(
@@ -284,6 +302,7 @@
                 (rate_hbm, rate_ref),
                 (gate_hbm, gate_ref),
                 (cache_hbm, cache_ref),
+                (gain_hbm, gain_ref),
             )
         )
     ]
@@ -305,6 +324,8 @@
     for load in weight_loads:
         load.start()
 
+    for ask in asks:
+        ask.wait()
     lane = iota((8, 128), 1)
     block = jnp.zeros((8, 128), jnp.int32)
     for part, ref in enumerate((owner_ref, node_ref, prefix_ref, slot_ref)):
@@ -312,9 +333,6 @@
             block = jnp.where(lane == part * requests + i, ref[i], block)
     info_ref[...] = block
 
-    barrier = pltpu.get_barrier_semaphore()
-    for device in near + [(worker, index) for index in others]:
-        pl.semaphore_signal(barrier, inc=1, device_id=device, device_id_type=MESH)
     pl.semaphore_wait(barrier, len(near) + len(others))
 
     def opposite(n):
@@ -365,20 +383,29 @@
             got_end_ref.at[2 + way, i], got_end_ref.at[way, i], end_send.at[way, i], end_recv.at[way, i], near[2 + way]
         )
 
-    def send_normed(kind, i):
+    def rows(way):
+        return pl.ds(way * half, half)
+
+    def send_normed(kind, i, way):
         source = 2 if kind == CROSS else 0
-        index = sides[i % 2][MATE] if kind == MATE else twin
+        index = sides[way][MATE] if kind == MATE else twin
         return remote(
-            normed_ref.at[i, source],
-            normed_ref.at[i, kind + 1],
-            normed_send.at[kind, i],
-            normed_recv.at[kind, i],
+            normed_ref.at[i, source, rows(way)],
+            normed_ref.at[i, kind + 1, rows(way)],
+            normed_send.at[kind, i, way],
+            normed_recv.at[kind, i, way],
             (worker, index),
         )
 
-    def send_partial(i):
-        index = sides[1 - i % 2][MATE]
-        return remote(passed_ref.at[i], got_ref.at[i], partial_send.at[i], partial_recv.at[i], (worker, index))
+    def send_partial(i, way):
+        index = sides[1 - way][MATE]
+        return remote(
+            passed_ref.at[i, rows(way)],
+            got_ref.at[i, rows(way)],
+            partial_send.at[i, way],
+            partial_recv.at[i, way],
+            (worker, index),
+        )
 
     def wanted(n, i):
         return cache_ref[jnp.clip(told_smem[n, 0, requests + i], 0, slots - 1)].astype(jnp.bfloat16)
@@ -419,8 +446,9 @@
         for h in range(heads):
             normed_ref[i, 0, :, h * DV : (h + 1) * DV] = normed[h]
             sent_end_ref[i, h] = ends[h].astype(jnp.bfloat16)
-        send_normed(MATE, i).start()
-        send_normed(TWIN, i).start()
+        for kind in (MATE, TWIN):
+            for way in range(2):
+                send_normed(kind, i, way).start()
         for way in range(2):
             send_end(way, i).start()
 
@@ -430,25 +458,29 @@
             pass_end(way, i).start()
 
     def forward(i):
-        send_normed(MATE, i).wait_recv()
-        send_normed(CROSS, i).start()
+        for way in range(2):
+            send_normed(MATE, i, way).wait_recv()
+            send_normed(CROSS, i, way).start()
 
     def project(i):
-        send_normed(TWIN, i).wait_recv()
-        send_normed(CROSS, i).wait_recv()
-        way = i % 2
-        total = dot1(normed_ref[i, 0], weight_ref[way, 0])
-        for source in range(1, 4):
-            total = total + dot1(normed_ref[i, source], weight_ref[way, source])
-        kept_ref[i] = total[:, :width]
-        passed_ref[i] = total[:, width:].astype(jnp.bfloat16)
-        send_partial(i).start()
+        for way in range(2):
+            send_normed(TWIN, i, way).wait_recv()
+            send_normed(CROSS, i, way).wait_recv()
+            total = dot1(normed_ref[i, 0, rows(way)], weight_ref[way, 0])
+            for source in range(1, 4):
+                total = total + dot1(normed_ref[i, source, rows(way)], weight_ref[way, source])
+            kept_ref[i, rows(way)] = total[:, :width]
+            passed_ref[i, rows(way)] = total[:, width:].astype(jnp.bfloat16)
+            send_partial(i, way).start()
 
     def add(i):
-        send_partial(i).wait_recv()
-        mixed_ref[i] = (kept_ref[i] + got_ref[i].astype(jnp.float32)).astype(jnp.bfloat16)
-
-    for load in loads[:6]:
+        for way in range(2):
+            send_partial(i, way).wait_recv()
+            mixed_ref[i, rows(way)] = (kept_ref[i, rows(way)] + got_ref[i, rows(way)].astype(jnp.float32)).astype(
+                jnp.bfloat16
+            )
+
+    for load in loads[:6] + loads[7:]:
         load.wait()
 
     def ready(rs, between):
@@ -472,14 +504,14 @@
         load.wait()
     for copy in weights:
         copy.wait_recv()
+    forward(0)
     relay(0)
-    forward(0)
-    relay(1)
     forward(1)
     project(0)
+    relay(1)
+    forward(2)
     relay(2)
     project(1)
-    forward(2)
     relay(3)
     forward(3)
     project(2)
@@ -487,6 +519,7 @@
     add(0)
     add(1)
     add(2)
+    add(3)
     for i in range(requests):
         for way in range(2):
             pass_end(way, i).wait_recv()
@@ -503,7 +536,6 @@
         end_ref[target] = jnp.where(
             kept, sent_end_ref[mine], got_end_ref[theirs // requests, theirs % requests]
         )
-    add(3)
 
     for copy in infos + weights:
         copy.wait_send()
@@ -513,9 +545,10 @@
             lend(way, i).wait_send()
             send_end(way, i).wait_send()
             pass_end(way, i).wait_send()
-        for kind in (TWIN, MATE, CROSS):
-            send_normed(kind, i).wait_send()
-        send_partial(i).wait_send()
+        for way in range(2):
+            for kind in (TWIN, MATE, CROSS):
+                send_normed(kind, i, way).wait_send()
+            send_partial(i, way).wait_send()
 
 
 def store_kernel(mixed_ref, end_ref, mixed_hbm, end_hbm, wide_ref, mixed_sem, end_sem):
@@ -550,7 +583,6 @@
     heads = log_decay.shape[1]
     width = heads * DV
     state = cache_states.shape[1:]
-    smem = pl.BlockSpec(memory_space=pltpu.SMEM)
     vmem = pl.BlockSpec(memory_space=pltpu.VMEM)
     anywhere = pl.BlockSpec(memory_space=pltpu.HBM)
     low, wide = jnp.bfloat16, jnp.float32
@@ -561,9 +593,11 @@
             pltpu.VMEM((requests, tokens, width), low),
             pltpu.VMEM((requests, *state), low),
         ),
-        in_specs=[smem] * 4 + [vmem] + [anywhere] * 8,
+        in_specs=[anywhere] * 13,
         out_specs=(vmem, vmem),
         scratch_shapes=[
+            *[pltpu.SMEM((requests,), jnp.int32)] * 4,
+            pltpu.VMEM((1, DV), wide),
             pltpu.VMEM(queries.shape, low),
             pltpu.VMEM(key_heads.shape, low),
             pltpu.VMEM(values_in.shape, low),
@@ -589,7 +623,8 @@
             pltpu.VMEM((requests, tokens, width), wide),
             pltpu.VMEM((requests, tokens, width), low),
             pltpu.VMEM((requests, tokens, width), low),
-            dma((7,)),
+            dma((4,)),
+            dma((8,)),
             dma((2, 2)),
             dma,
             dma((4,)),
@@ -602,10 +637,10 @@
             dma((4, requests)),
             dma((2, 3, 2)),
             dma((2, 3, 2)),
-            dma((3, requests)),
-            dma((3, requests)),
-            dma((requests,)),
-            dma((requests,)),
+            dma((3, requests, 2)),
+            dma((3, requests, 2)),
+            dma((requests, 2)),
+            dma((requests, 2)),
         ],
         compiler_params=pltpu.CompilerParams(
             collective_id=0, has_side_effects=True, vmem_limit_bytes=48 * 1024 * 1024

time: 51.8 us -> 50.2 us (0.969)
  Pallas kernels: 51 us -> 49.5 us
    pallas_call x1, Pallas kernels: 50 us -> 48.4 us  [on_device(): pl.pallas_call(functools.partial(layer_kernel, lax.axis_size('worker')),...]
where the time goes in v4:
time: 50.2 us; the launch traced here: 50.1 us
  Pallas kernels  49.5 us (99%)
  between operations  0.64 us (1%)
    pallas_call x1, Pallas kernels, on_device(): pl.pallas_call(functools.partial(layer_kernel, lax.axis_size('worker')),...  48.4 us
    pallas_call x1, Pallas kernels, on_device(): pl.pallas_call(store_kernel, out_shape=(jax.ShapeDtypeStruct(mixed.shape,...  1.03 us

profile of v4, /device:TPU:1, one launch (start us, length us, event | category | flops | bytes accessed | tf_op | source)
XLA Modules:
  0.0 50.1 jit_solution(605469265347580695)
XLA Ops:
  0.6 48.4 %layer.1 = (bf16[4,256,256]{2,1,0:T(8,128)(2,1)S(1)}, bf16[4,2,128,128]{3,2,1,0:T(8,128)(2,1)S(1)}) custom-call(s32[4]{0:T(128)} %owner_hbm.1, s32[4]{0:T(128)} %node_hbm.1, s32[4]{0:T(128)} %prefix_hbm.1, s32[4]{0:T(128)} %slot_hbm.1, f32[1,128]{1,0:T(1,128)} %bitcast.1, bf16[4,256,128]{2,1,0:T(8,128)(2,1)} %q_hbm.1, bf16[4,256,128]{2,1,0:T(8,128)(2,1)} %k_hbm.1, ...), custom_call_target="tpu_custom_call" | custom-call | tf_op jit(solution)/shard_map/layer/pallas_call | solution.py:590
  49.1 1.0 %store.1 = (bf16[4,256,256]{2,1,0:T(8,128)(2,1)}, f32[4,2,128,128]{3,2,1,0:T(8,128)}) custom-call(bf16[4,256,256]{2,1,0:T(8,128)(2,1)S(1)} %get-tuple-element.4.mixed_ref, bf16[4,2,128,128]{3,2,1,0:T(8,128)(2,1)S(1)} %get-tuple-element.5.end_ref), custom_call_target="tpu_custom_call" | custom-call | tf_op jit(solution)/shard_map/store/pallas_call | solution.py:669

commit v5 on v4

--- a/solution.py
+++ b/solution.py
@@ -13,7 +13,7 @@
 SMALL = 8
 MESH = pl.DeviceIdType.MESH
 OFFSETS = (-2, 2, -1, 1)
-TWIN, MATE, CROSS = range(3)
+TWIN = 0
 
 
 def split(x):
@@ -234,9 +234,12 @@
     got_end_ref,
     weight_ref,
     normed_ref,
+    gathered_ref,
     kept_ref,
     passed_ref,
     got_ref,
+    lent_sum_ref,
+    twin_sum_ref,
     ask_sem,
     load_sem,
     weight_load_sem,
@@ -255,6 +258,8 @@
     normed_recv,
     partial_send,
     partial_recv,
+    swap_send,
+    swap_recv,
 ):
     requests, tokens = q_ref.shape[:2]
     half = tokens // 2
@@ -265,15 +270,13 @@
     tensor = lax.axis_index("tensor")
     chip, core = tensor // 2, tensor % 2
 
-    def paired(index, way):
-        there = index // 2
-        mate = 3 - there if way else there + 1 - 2 * (there % 2)
-        return 2 * mate + index % 2
+    def paired(there, way):
+        return (1 - way) * (there + 1 - 2 * (there % 2)) + way * (3 - there)
 
     near = [(lax.rem(worker + workers + o, workers), tensor) for o in OFFSETS]
     twin = 2 * chip + 1 - core
-    sides = [(twin, paired(tensor, way), paired(twin, way)) for way in range(2)]
-    others = [twin, *sides[0][1:], *sides[1][1:]]
+    others = [twin] + [2 * paired(chip, way) + c for way in range(2) for c in range(2)]
+    beyond = paired(chip, 1 - core)
 
     def remote(src, dst, send, recv, device):
         return pltpu.make_async_remote_copy(
@@ -309,17 +312,19 @@
     for load in loads:
         load.start()
 
-    def columns(index):
-        return pl.ds(pl.multiple_of(index * width, width), width)
+    def columns(there):
+        return pl.ds(pl.multiple_of(there * 2 * width, 2 * width), 2 * width)
+
+    def rows(c):
+        return pl.ds(pl.multiple_of(c * half, half), half)
 
     weight_loads = [
         pltpu.make_async_copy(
-            proj_hbm.at[:, columns(index)],
-            weight_ref.at[way, 0, :, pl.ds(part * width, width)],
-            weight_load_sem.at[way, part],
-        )
-        for way in range(2)
-        for part, index in enumerate((tensor, paired(tensor, 1 - way)))
+            proj_hbm.at[:, columns(there)],
+            weight_ref.at[0, :, pl.ds(part * 2 * width, 2 * width)],
+            weight_load_sem.at[part],
+        )
+        for part, there in enumerate((chip, beyond))
     ]
     for load in weight_loads:
         load.start()
@@ -345,21 +350,37 @@
     for copy in infos:
         copy.start()
 
+    def route(kind):
+        if kind == TWIN:
+            return twin, 1, 1 - core, chip
+        way = kind - 1
+        there = paired(chip, way)
+        return 2 * there + way, 2 + lax.rem(core + way, 2), way, there
+
     weights = []
-    for kind in (MATE, CROSS, TWIN):
-        for part in range(2):
-            for way in range(2):
-                index = sides[way][kind]
-                target = paired(index, 1 - way) if part else index
-                weights.append(
-                    remote(
-                        proj_hbm.at[:, columns(target)],
-                        weight_ref.at[way, kind + 1, :, pl.ds(part * width, width)],
-                        weight_send.at[way, kind, part],
-                        weight_recv.at[way, kind, part],
-                        (worker, index),
-                    )
+    for kind in (1, 2, TWIN):
+        index, source, way, there = route(kind)
+        for part, block in enumerate((there, paired(there, 1 - way))):
+            weights.append(
+                remote(
+                    proj_hbm.at[:, columns(block)],
+                    weight_ref.at[source, :, pl.ds(part * 2 * width, 2 * width)],
+                    weight_send.at[kind, part],
+                    weight_recv.at[source - 1, part],
+                    (worker, index),
                 )
+            )
+    got_weights = [
+        remote(
+            proj_hbm.at[:, columns(chip)],
+            weight_ref.at[source, :, pl.ds(part * 2 * width, 2 * width)],
+            weight_send.at[source - 1, part],
+            weight_recv.at[source - 1, part],
+            (worker, twin),
+        )
+        for source in range(1, 4)
+        for part in range(2)
+    ]
     for copy in weights:
         copy.start()
 
@@ -383,29 +404,41 @@
             got_end_ref.at[2 + way, i], got_end_ref.at[way, i], end_send.at[way, i], end_recv.at[way, i], near[2 + way]
         )
 
-    def rows(way):
-        return pl.ds(way * half, half)
-
-    def send_normed(kind, i, way):
-        source = 2 if kind == CROSS else 0
-        index = sides[way][MATE] if kind == MATE else twin
+    def send_normed(kind, i):
+        index, source, way, _ = route(kind)
         return remote(
-            normed_ref.at[i, source, rows(way)],
-            normed_ref.at[i, kind + 1, rows(way)],
-            normed_send.at[kind, i, way],
-            normed_recv.at[kind, i, way],
+            normed_ref.at[i, rows(way)],
+            gathered_ref.at[i, source - 1],
+            normed_send.at[kind, i],
+            normed_recv.at[source - 1, i],
             (worker, index),
         )
 
-    def send_partial(i, way):
-        index = sides[1 - way][MATE]
+    def get_normed(source, i):
         return remote(
-            passed_ref.at[i, rows(way)],
-            got_ref.at[i, rows(way)],
-            partial_send.at[i, way],
-            partial_recv.at[i, way],
-            (worker, index),
-        )
+            normed_ref.at[i, rows(core)],
+            gathered_ref.at[i, source - 1],
+            normed_send.at[source - 1, i],
+            normed_recv.at[source - 1, i],
+            (worker, twin),
+        )
+
+    def send_partial(i, c):
+        return remote(
+            passed_ref.at[i, c],
+            got_ref.at[i, rows(core)],
+            partial_send.at[i, c],
+            partial_recv.at[i, core],
+            (worker, 2 * beyond + c),
+        )
+
+    def get_partial(i, c):
+        return remote(
+            passed_ref.at[i, c], got_ref.at[i, rows(c)], partial_send.at[i, c], partial_recv.at[i, c], (worker, twin)
+        )
+
+    def swap(i):
+        return remote(lent_sum_ref.at[i], twin_sum_ref.at[i], swap_send.at[i], swap_recv.at[i], (worker, twin))
 
     def wanted(n, i):
         return cache_ref[jnp.clip(told_smem[n, 0, requests + i], 0, slots - 1)].astype(jnp.bfloat16)
@@ -420,7 +453,8 @@
         for i in range(requests):
             for way in range(2):
                 hop_out_ref[way, i] = wanted(way, i)
-                hop(way, i).start()
+                if i < requests - 1:
+                    hop(way, i).start()
 
     def merge(i):
         for way in range(2):
@@ -444,11 +478,10 @@
         slots_here = [i * heads + h for h in range(heads)]
         normed, ends = finish(slots_here, starts, zhi_ref, zlo_ref, base_ref, gain_gate_ref)
         for h in range(heads):
-            normed_ref[i, 0, :, h * DV : (h + 1) * DV] = normed[h]
+            normed_ref[i, :, h * DV : (h + 1) * DV] = normed[h]
             sent_end_ref[i, h] = ends[h].astype(jnp.bfloat16)
-        for kind in (MATE, TWIN):
-            for way in range(2):
-                send_normed(kind, i, way).start()
+        for kind in (1, 2, TWIN):
+            send_normed(kind, i).start()
         for way in range(2):
             send_end(way, i).start()
 
@@ -457,26 +490,25 @@
             send_end(way, i).wait_recv()
             pass_end(way, i).start()
 
-    def forward(i):
-        for way in range(2):
-            send_normed(MATE, i, way).wait_recv()
-            send_normed(CROSS, i, way).start()
-
     def project(i):
-        for way in range(2):
-            send_normed(TWIN, i, way).wait_recv()
-            send_normed(CROSS, i, way).wait_recv()
-            total = dot1(normed_ref[i, 0, rows(way)], weight_ref[way, 0])
-            for source in range(1, 4):
-                total = total + dot1(normed_ref[i, source, rows(way)], weight_ref[way, source])
-            kept_ref[i, rows(way)] = total[:, :width]
-            passed_ref[i, rows(way)] = total[:, width:].astype(jnp.bfloat16)
-            send_partial(i, way).start()
+        total = dot1(normed_ref[i, rows(core)], weight_ref[0])
+        for source in range(1, 4):
+            get_normed(source, i).wait_recv()
+            total = total + dot1(gathered_ref[i, source - 1], weight_ref[source])
+        for c in range(2):
+            passed_ref[i, c] = total[:, (2 + c) * width : (3 + c) * width].astype(jnp.bfloat16)
+            send_partial(i, c).start()
+        left, right = total[:, :width], total[:, width : 2 * width]
+        lent_sum_ref[i] = jnp.where(core == 0, right, left).astype(jnp.bfloat16)
+        swap(i).start()
+        kept_ref[i] = jnp.where(core == 0, left, right)
 
     def add(i):
-        for way in range(2):
-            send_partial(i, way).wait_recv()
-            mixed_ref[i, rows(way)] = (kept_ref[i, rows(way)] + got_ref[i, rows(way)].astype(jnp.float32)).astype(
+        swap(i).wait_recv()
+        for c in range(2):
+            get_partial(i, c).wait_recv()
+        for sums, c in ((kept_ref, core), (twin_sum_ref, 1 - core)):
+            mixed_ref[i, rows(c)] = (sums[i].astype(jnp.float32) + got_ref[i, rows(c)].astype(jnp.float32)).astype(
                 jnp.bfloat16
             )
 
@@ -490,6 +522,8 @@
 
     def merge_first():
         merge(0)
+        for way in range(2):
+            hop(way, requests - 1).start()
         merge(1)
 
     ready([0, 1], answer)
@@ -499,23 +533,19 @@
     complete(0)
     complete(1)
     complete(2)
-    complete(3)
     for load in weight_loads:
         load.wait()
-    for copy in weights:
+    for copy in got_weights:
         copy.wait_recv()
-    forward(0)
+    project(0)
+    complete(3)
     relay(0)
-    forward(1)
-    project(0)
+    project(1)
     relay(1)
-    forward(2)
+    project(2)
     relay(2)
-    project(1)
+    project(3)
     relay(3)
-    forward(3)
-    project(2)
-    project(3)
     add(0)
     add(1)
     add(2)
@@ -545,10 +575,11 @@
             lend(way, i).wait_send()
             send_end(way, i).wait_send()
             pass_end(way, i).wait_send()
-        for way in range(2):
-            for kind in (TWIN, MATE, CROSS):
-                send_normed(kind, i, way).wait_send()
-            send_partial(i, way).wait_send()
+        for kind in range(3):
+            send_normed(kind, i).wait_send()
+        for c in range(2):
+            send_partial(i, c).wait_send()
+        swap(i).wait_send()
 
 
 def store_kernel(mixed_ref, end_ref, mixed_hbm, end_hbm, wide_ref, mixed_sem, end_sem):
@@ -618,14 +649,17 @@
             pltpu.VMEM((2, requests, *state), low),
             pltpu.VMEM((requests, *state), low),
             pltpu.VMEM((4, requests, *state), low),
-            pltpu.VMEM((2, 4, width, 2 * width), low),
-            pltpu.VMEM((requests, 4, tokens, width), low),
-            pltpu.VMEM((requests, tokens, width), wide),
+            pltpu.VMEM((4, width, 4 * width), low),
             pltpu.VMEM((requests, tokens, width), low),
+            pltpu.VMEM((requests, 3, tokens // 2, width), low),
+            pltpu.VMEM((requests, tokens // 2, width), wide),
+            pltpu.VMEM((requests, 2, tokens // 2, width), low),
             pltpu.VMEM((requests, tokens, width), low),
+            pltpu.VMEM((requests, tokens // 2, width), low),
+            pltpu.VMEM((requests, tokens // 2, width), low),
             dma((4,)),
             dma((8,)),
-            dma((2, 2)),
+            dma((2,)),
             dma,
             dma((4,)),
             dma((4,)),
@@ -635,12 +669,14 @@
             dma((2, requests)),
             dma((4, requests)),
             dma((4, requests)),
-            dma((2, 3, 2)),
-            dma((2, 3, 2)),
-            dma((3, requests, 2)),
-            dma((3, requests, 2)),
+            dma((3, 2)),
+            dma((3, 2)),
+            dma((3, requests)),
+            dma((3, requests)),
             dma((requests, 2)),
             dma((requests, 2)),
+            dma((requests,)),
+            dma((requests,)),
         ],
         compiler_params=pltpu.CompilerParams(
             collective_id=0, has_side_effects=True, vmem_limit_bytes=48 * 1024 * 1024

time: 50.2 us -> 49.2 us (0.980)
  Pallas kernels: 49.5 us -> 48.5 us
    pallas_call x1, Pallas kernels: 48.4 us -> 47.5 us  [on_device(): pl.pallas_call(functools.partial(layer_kernel, lax.axis_size('worker')),...]
where the time goes in v5:
time: 49.2 us; the launch traced here: 49.1 us
  Pallas kernels  48.5 us (99%)
  between operations  0.64 us (1%)
    pallas_call x1, Pallas kernels, on_device(): pl.pallas_call(functools.partial(layer_kernel, lax.axis_size('worker')),...  47.5 us
    pallas_call x1, Pallas kernels, on_device(): pl.pallas_call(store_kernel, out_shape=(jax.ShapeDtypeStruct(mixed.shape,...  1.03 us

profile of v5, /device:TPU:1, one launch (start us, length us, event | category | flops | bytes accessed | tf_op | source)
XLA Modules:
  0.0 49.1 jit_solution(12527710127940067996)
XLA Ops:
  0.6 47.5 %layer.1 = (bf16[4,256,256]{2,1,0:T(8,128)(2,1)S(1)}, bf16[4,2,128,128]{3,2,1,0:T(8,128)(2,1)S(1)}) custom-call(s32[4]{0:T(128)} %owner_hbm.1, s32[4]{0:T(128)} %node_hbm.1, s32[4]{0:T(128)} %prefix_hbm.1, s32[4]{0:T(128)} %slot_hbm.1, f32[1,128]{1,0:T(1,128)} %bitcast.1, bf16[4,256,128]{2,1,0:T(8,128)(2,1)} %q_hbm.1, bf16[4,256,128]{2,1,0:T(8,128)(2,1)} %k_hbm.1, ...), custom_call_target="tpu_custom_call" | custom-call | tf_op jit(solution)/shard_map/layer/pallas_call | solution.py:621
  48.1 1.0 %store.1 = (bf16[4,256,256]{2,1,0:T(8,128)(2,1)}, f32[4,2,128,128]{3,2,1,0:T(8,128)}) custom-call(bf16[4,256,256]{2,1,0:T(8,128)(2,1)S(1)} %get-tuple-element.4.mixed_ref, bf16[4,2,128,128]{3,2,1,0:T(8,128)(2,1)S(1)} %get-tuple-element.5.end_ref), custom_call_target="tpu_custom_call" | custom-call | tf_op jit(solution)/shard_map/store/pallas_call | solution.py:705

commit v6 on v5

--- a/solution.py
+++ b/solution.py
@@ -450,11 +450,11 @@
         fetch.start()
         fetch.wait()
         loads[6].wait()
-        for i in range(requests):
+        @pl.loop(0, requests)
+        def _(i):
             for way in range(2):
                 hop_out_ref[way, i] = wanted(way, i)
-                if i < requests - 1:
-                    hop(way, i).start()
+                hop(way, i).start()
 
     def merge(i):
         for way in range(2):
@@ -521,35 +521,23 @@
         )
 
     def merge_first():
-        merge(0)
-        for way in range(2):
-            hop(way, requests - 1).start()
-        merge(1)
+        pl.loop(0, 2)(merge)
 
     ready([0, 1], answer)
     ready([2, 3], merge_first)
-    merge(2)
-    merge(3)
-    complete(0)
-    complete(1)
-    complete(2)
+    pl.loop(2, requests)(merge)
+    pl.loop(0, requests)(complete)
     for load in weight_loads:
         load.wait()
     for copy in got_weights:
         copy.wait_recv()
-    project(0)
-    complete(3)
-    relay(0)
-    project(1)
-    relay(1)
-    project(2)
-    relay(2)
-    project(3)
-    relay(3)
-    add(0)
-    add(1)
-    add(2)
-    add(3)
+
+    @pl.loop(0, requests)
+    def _(i):
+        project(i)
+        relay(i)
+
+    pl.loop(0, requests)(add)
     for i in range(requests):
         for way in range(2):
             pass_end(way, i).wait_recv()

time: 49.2 us -> 48.6 us (0.988)
  Pallas kernels: 48.5 us -> 47.9 us
    pallas_call x1, Pallas kernels: 47.5 us -> 46.9 us  [on_device(): pl.pallas_call(functools.partial(layer_kernel, lax.axis_size('worker')),...]
where the time goes in v6:
time: 48.6 us; the launch traced here: 48.5 us
  Pallas kernels  47.9 us (99%)
  between operations  0.64 us (1%)
    pallas_call x1, Pallas kernels, on_device(): pl.pallas_call(functools.partial(layer_kernel, lax.axis_size('worker')),...  46.9 us
    pallas_call x1, Pallas kernels, on_device(): pl.pallas_call(store_kernel, out_shape=(jax.ShapeDtypeStruct(mixed.shape,...  1.03 us

profile of v6, /device:TPU:1, one launch (start us, length us, event | category | flops | bytes accessed | tf_op | source)
XLA Modules:
  0.0 48.5 jit_solution(9846433202434994526)
XLA Ops:
  0.6 46.9 %layer.1 = (bf16[4,256,256]{2,1,0:T(8,128)(2,1)S(1)}, bf16[4,2,128,128]{3,2,1,0:T(8,128)(2,1)S(1)}) custom-call(s32[4]{0:T(128)} %owner_hbm.1, s32[4]{0:T(128)} %node_hbm.1, s32[4]{0:T(128)} %prefix_hbm.1, s32[4]{0:T(128)} %slot_hbm.1, f32[1,128]{1,0:T(1,128)} %bitcast.1, bf16[4,256,128]{2,1,0:T(8,128)(2,1)} %q_hbm.1, bf16[4,256,128]{2,1,0:T(8,128)(2,1)} %k_hbm.1, ...), custom_call_target="tpu_custom_call" | custom-call | tf_op jit(solution)/shard_map/layer/pallas_call | solution.py:609
  47.5 1.0 %store.1 = (bf16[4,256,256]{2,1,0:T(8,128)(2,1)}, f32[4,2,128,128]{3,2,1,0:T(8,128)}) custom-call(bf16[4,256,256]{2,1,0:T(8,128)(2,1)S(1)} %get-tuple-element.4.mixed_ref, bf16[4,2,128,128]{3,2,1,0:T(8,128)(2,1)S(1)} %get-tuple-element.5.end_ref), custom_call_target="tpu_custom_call" | custom-call | tf_op jit(solution)/shard_map/store/pallas_call | solution.py:693

commit v7 on v6

--- a/solution.py
+++ b/solution.py
@@ -520,11 +520,17 @@
             rs, between, q_ref, k_ref, v_ref, gate_ref, decay_ref, rate_ref, gain_ref, zhi_ref, zlo_ref, base_ref, gain_gate_ref
         )
 
-    def merge_first():
-        pl.loop(0, 2)(merge)
-
-    ready([0, 1], answer)
-    ready([2, 3], merge_first)
+    @pl.loop(0, requests // 2)
+    def _(pair):
+        def between():
+            pl.when(pair == 0)(answer)
+
+            @pl.when(pair == 1)
+            def _():
+                pl.loop(0, 2)(merge)
+
+        ready([2 * pair, 2 * pair + 1], between)
+
     pl.loop(2, requests)(merge)
     pl.loop(0, requests)(complete)
     for load in weight_loads:

time: 48.6 us -> 48.8 us (level)
  no operation moved by 1% of the time
where the time goes in v7:
time: 48.8 us; the launch traced here: 48.7 us
  Pallas kernels  48.1 us (99%)
  between operations  0.64 us (1%)
    pallas_call x1, Pallas kernels, on_device(): pl.pallas_call(functools.partial(layer_kernel, lax.axis_size('worker')),...  47 us
    pallas_call x1, Pallas kernels, on_device(): pl.pallas_call(store_kernel, out_shape=(jax.ShapeDtypeStruct(mixed.shape,...  1.03 us

profile of v7, /device:TPU:1, one launch (start us, length us, event | category | flops | bytes accessed | tf_op | source)
XLA Modules:
  0.0 48.7 jit_solution(14955372088679386503)
XLA Ops:
  0.6 47.0 %layer.1 = (bf16[4,256,256]{2,1,0:T(8,128)(2,1)S(1)}, bf16[4,2,128,128]{3,2,1,0:T(8,128)(2,1)S(1)}) custom-call(s32[4]{0:T(128)} %owner_hbm.1, s32[4]{0:T(128)} %node_hbm.1, s32[4]{0:T(128)} %prefix_hbm.1, s32[4]{0:T(128)} %slot_hbm.1, f32[1,128]{1,0:T(1,128)} %bitcast.1, bf16[4,256,128]{2,1,0:T(8,128)(2,1)} %q_hbm.1, bf16[4,256,128]{2,1,0:T(8,128)(2,1)} %k_hbm.1, ...), custom_call_target="tpu_custom_call" | custom-call | tf_op jit(solution)/shard_map/layer/pallas_call | solution.py:615
  47.7 1.0 %store.1 = (bf16[4,256,256]{2,1,0:T(8,128)(2,1)}, f32[4,2,128,128]{3,2,1,0:T(8,128)}) custom-call(bf16[4,256,256]{2,1,0:T(8,128)(2,1)S(1)} %get-tuple-element.4.mixed_ref, bf16[4,2,128,128]{3,2,1,0:T(8,128)(2,1)S(1)} %get-tuple-element.5.end_ref), custom_call_target="tpu_custom_call" | custom-call | tf_op jit(solution)/shard_map/store/pallas_call | solution.py:699
